TPU v7x, 128 devices: a whole 4x4x4 slice. The times are simulated.
128 devices in a mesh: row: 8 (over z, core), col: 16 (over y, x).
Axes of the slice: x: 4, y: 4, z: 4, core: 2. Of those that a mesh axis runs over, the one named last changes fastest.
Arguments:
- inputs: bfloat16 [8192, 2048], P('row', 'col'), may hold values from -6 to 6
- seq_lengths: int32 [8, 2], P('row'), may hold values from 256 to 768, as said below
- query_key_value_weight: bfloat16 [2048, 3, 2048], P('row', None, 'col'), may hold values from -0.125 to 0.125
- query_key_value_bias: bfloat16 [3, 2048], P(None, ('col', 'row')), may hold values from -1.796875 to 1.796875
- w_out: bfloat16 [2048, 2048], P('col', 'row'), may hold values from -2 to 2
- b_out: bfloat16 [2048], P(('col', 'row')), may hold values from -1.796875 to 1.796875
- w_up: bfloat16 [2048, 8192], P('row', 'col'), may hold values from -0.125 to 0.125
- b_up: bfloat16 [8192], P(('col', 'row')), may hold values from -1.796875 to 1.796875
- w_down: bfloat16 [8192, 2048], P('col', 'row'), may hold values from -0.0625 to 0.0625
- b_down: bfloat16 [2048], P(('col', 'row')), may hold values from -1.796875 to 1.796875
- ln_gain: bfloat16 [2048], P(('col', 'row')), may hold values from 0.5 to 1.5
- ln_bias: bfloat16 [2048], P(('col', 'row')), may hold values from -1.796875 to 1.796875
- cotangent: bfloat16 [8192, 2048], P('row', 'col'), may hold values from -6 to 6
Outputs:
- block_out: bfloat16 [8192, 2048], P('row', 'col')
- input_grad: float32 [8192, 2048], P('row', 'col')
- query_key_value_gradient: float32 [2048, 3, 2048], P('row', None, 'col')
- grad_qkv_bias: float32 [3, 2048], P(None, ('col', 'row'))
- grad_out: float32 [2048, 2048], P('col', 'row')
- grad_out_bias: float32 [2048], P(('col', 'row'))
- grad_up: float32 [2048, 8192], P('row', 'col')
- grad_up_bias: float32 [8192], P(('col', 'row'))
- grad_down: float32 [8192, 2048], P('col', 'row')
- grad_down_bias: float32 [2048], P(('col', 'row'))
- grad_ln_gain: float32 [2048], P(('col', 'row'))
- grad_ln_bias: float32 [2048], P(('col', 'row'))
Inputs may be any that keep to these rules, and one draw needn't show every extreme that they name: `seq_lengths`: row r holds the lengths of the 2 sequences of group r in order; in every row one length is 768 and the other 256, in either order.
All inputs are finite; a program needn't handle non-finite values.
Results may differ from a plain program's by a relative error of at most 0.01.
Values may be sent and summed in bfloat16 or wider, within the bound.
No kernel may reach another device: no remote copies, remote signals or barrier semaphores. Data moves between devices by JAX's collectives and lax.ppermute only.
A program may use at most 128 MiB of HBM per device.

v0:
```python
import functools

import jax
import jax.numpy as jnp
from jax import lax
from jax.experimental import pallas as pl
from jax.experimental.pallas import tpu as pltpu
from jax.sharding import PartitionSpec as P

D = 2048
HEAD_DIM = 64
ROT = 32
EPS = 1e-05
TOK = 1024
HALF = 512
QKV = 384
FFL = 512
CAT = QKV + FFL
ACT = 128 + FFL
ALL = CAT + ACT
PAD = 16
BLK = 256
F32 = jnp.float32
BF16 = jnp.bfloat16
MIB = 2**20

MASKS = ((1, 3, 2), (3, 1, 2))


def exchange(value, axis, step=0):
    pairs = []
    for z in range(4):
        for k in range(2):
            m = MASKS[k][step]
            for y in range(4):
                for x in range(4):
                    to = {
                        "x": (x ^ m, y, z, k),
                        "y": (x, y ^ m, z, k),
                        "z": (x, y, z ^ m, k),
                        "c": (x, y, z, 1 - k),
                    }[axis]
                    pairs.append(((z * 2 + k) * 16 + y * 4 + x, (to[2] * 2 + to[3]) * 16 + to[1] * 4 + to[0]))
    return lax.ppermute(value, ("row", "col"), pairs)


PIECE_OF = [(i // 8, i % 8) for i in range(16)]
ROW_PIECES = (4, 4)
NN = ((1,), (0,))
NT = ((1,), (1,))
TN = ((0,), (0,))


def dot(a, b, dims):
    return lax.dot_general(a, b, (dims, ((), ())), preferred_element_type=F32)


def weight_blocks(refs):
    first = 0
    for n, ref in zip(ROW_PIECES, refs):
        yield first, n, ref
        first += n


def weight_of(refs, j):
    for first, n, ref in weight_blocks(refs):
        if first <= j < first + n:
            return ref.at[j - first]


def gelu_tanh_part(v):
    return jnp.tanh(0.7978845608028654 * (v + 0.044715 * v * v * v))


class Place:
    def __init__(self):
        row, col = lax.axis_index("row"), lax.axis_index("col")
        self.row = row
        self.z, self.core, self.y, self.x = lax.div(row, 2), lax.rem(row, 2), lax.div(col, 4), lax.rem(col, 4)
        self.m1 = jnp.where(self.core == 0, 1, 3)
        self.m2 = 4 - self.m1
        self.seen = (0, self.m1, self.m2, 2)

    def swapped(self, mask):
        return jnp.where(mask == self.m2, 1, jnp.where(mask == self.m1, 2, jnp.where(mask == 2, 3, 0)))

    def lane(self, half, i):
        outer, inner = self.seen[i // 4], self.seen[i % 4]
        y, x = (self.y ^ outer, self.x ^ inner) if half == 0 else (self.y ^ inner, self.x ^ outer)
        owner = y * 2 + lax.div(x, 2)
        mask = lax.div(owner, 2) ^ self.z
        same = lax.rem(owner, 2) == self.core
        first = jnp.where(mask == self.m1, 1, jnp.where(mask == self.m2, 2, jnp.where(mask == 2, 3, 0)))
        block = jnp.where(same, first, 4 + self.swapped(mask))
        return pl.multiple_of((block * 2 + lax.rem(x, 2)) * 128, 128)

    def spot(self, half, j, i):
        if j < 4:
            z, core = self.z ^ self.seen[j], self.core
        else:
            z, core = self.z ^ (0, self.m2, self.m1, 2)[j - 4], 1 - self.core
        owner = (z * 2 + core) * 2 + i
        y, x = self.swapped(lax.div(owner, 4) ^ self.y), self.swapped(lax.rem(owner, 4) ^ self.x)
        return y * 4 + x if half == 0 else x * 4 + y


def vmem():
    return pl.BlockSpec(memory_space=pltpu.VMEM)


def smem():
    return pl.BlockSpec(memory_space=pltpu.SMEM)


def any_spec():
    return pl.BlockSpec(memory_space=pl.ANY)


def shape(dims, dtype):
    return jax.ShapeDtypeStruct(dims, dtype)


WORK = dict(norm_proj=9, attend=3, project=5, upstream=6, attend_back=7, downstream=6, grads=11)
VMEM_MIB = dict(norm_proj=7, attend=8, project=7, upstream=7, attend_back=11, downstream=8, grads=8)


def call(name, kernel, specs, outs, args, scratch=(), after=(), final=False):
    if after:
        body, n = kernel, len(args)
        kernel = lambda *refs: body(*refs[:n], *refs[n + len(after) :])
        specs = list(specs) + [any_spec()] * len(after)
    return pl.pallas_call(
        kernel,
        in_specs=specs,
        out_specs=[vmem()] * len(outs),
        out_shape=outs if final else [pltpu.VMEM(o.shape, o.dtype) for o in outs],
        scratch_shapes=list(scratch),
        compiler_params=pltpu.CompilerParams(vmem_limit_bytes=VMEM_MIB.get(name, 3) * MIB),
        cost_estimate=pl.CostEstimate(flops=int(WORK.get(name, 0) * 2.5e8), bytes_accessed=0, transcendentals=0),
        name=name,
    )(*args, *after)


def norm_kernel(*refs):
    place = Place()
    halves, tiny, wts = (refs[0:2], refs[2:4]), refs[4:6], refs[6:8]
    cos_ref, sa_ref, sb_ref = refs[8:11]
    normed_ref, qkv_ref, pre_ref, act_ref, cen_ref, inv_ref, gb_ref = refs[11:]

    lanes = [[place.lane(half, i) for i in range(16)] for half in range(2)]

    def lane(half, i):
        return lanes[half][i]

    def tiny_of(i):
        return PIECE_OF[(0, 2, 1, 3)[i // 4] * 4 + i % 4]

    def tiny_row(i, row):
        a, k = tiny_of(i)
        return tiny[a][k, row : row + 1, :].astype(F32)

    for i in range(16):
        a, k = tiny_of(i)
        gb_ref[:, pl.ds(lane(0, i), 128)] = tiny[a][k].astype(F32)[0:8]
    bias = jnp.concatenate([tiny_row(0, 4 + i) for i in range(7)], axis=1)

    for half in range(2):
        pieces = halves[half]

        def chunk(t, _, half=half, pieces=pieces):
            here = pl.ds(pl.multiple_of(t * 16, 16), 16)
            rows = pl.ds(pl.multiple_of(half * HALF + t * 16, 16), 16)
            xs = [pieces[a][k, here, :].astype(F32) for a, k in PIECE_OF]
            total = xs[0]
            square = xs[0] * xs[0]
            for x in xs[1:]:
                total = total + x
                square = square + x * x
            mean = jnp.sum(total, axis=1, keepdims=True) * (1.0 / D)
            square = jnp.sum(square, axis=1, keepdims=True) * (1.0 / D)
            inv = lax.rsqrt(square - mean * mean + EPS)
            for i, x in enumerate(xs):
                j = i if half == 0 else (i % 4) * 4 + i // 4
                centered = (x - mean) * inv
                if i == 0:
                    cen_ref[rows, :] = centered
                normed_ref[rows, pl.ds(lane(half, i), 128)] = (centered * tiny_row(j, 0) + tiny_row(j, 1)).astype(BF16)
            inv_ref[rows, :] = jnp.broadcast_to(inv, (16, 128))
            return _

        lax.fori_loop(0, HALF // 16, chunk, 0, unroll=4)

    @pl.loop(0, TOK // BLK)
    def _(t):
        rows = pl.ds(pl.multiple_of(t * BLK, BLK), BLK)
        mixed = bias
        for first, n, ref in weight_blocks(wts):
            lines = slice(first * BLK, (first + n) * BLK)
            mixed = mixed + dot(normed_ref[rows, lines], ref[...].reshape(n * BLK, CAT), NN)
        for s in range(2):
            v = mixed[:, s * 128 : (s + 1) * 128]
            v = v * cos_ref[rows, :] + pltpu.roll(v, 128 - 16, 1) * sa_ref[rows, :] + pltpu.roll(v, 16, 1) * sb_ref[rows, :]
            qkv_ref[rows, s * 128 : (s + 1) * 128] = v.astype(BF16)
        qkv_ref[rows, 256:384] = mixed[:, 256:384].astype(BF16)
        pre = mixed[:, QKV:CAT]
        pre_ref[rows, :] = pre
        act_ref[rows, :] = (0.5 * pre * (1.0 + gelu_tanh_part(pre))).astype(BF16)


def norm_call(xa, xb, tiny, wts, cos, sa, sb):
    outs = [
        shape((TOK, D), BF16),
        shape((TOK, QKV), BF16),
        shape((TOK, FFL), F32),
        shape((TOK, FFL), BF16),
        shape((TOK, 128), F32),
        shape((TOK, 128), F32),
        shape((8, D), F32),
    ]
    args = (*xa, *xb, *tiny, *wts, cos, sa, sb)
    return call("norm_proj", norm_kernel, [vmem()] * 11, outs, args)


def head_masks():
    lane = lax.broadcasted_iota(jnp.int32, (1, 128), 1)
    return [(lane < HEAD_DIM).astype(BF16), (lane >= HEAD_DIM).astype(BF16)]


def masked_scores(qh, k, qi):
    s = dot(qh, k, NT)
    row = lax.broadcasted_iota(jnp.int32, (BLK, BLK), 0)
    column = lax.broadcasted_iota(jnp.int32, (BLK, BLK), 1)
    last = jnp.where(row >= column, s[:, qi * BLK :], -1e30)
    return last if qi == 0 else jnp.concatenate([s[:, : qi * BLK], last], axis=1)


def for_blocks(lengths, body):
    long_first = lengths[0, 0] > lengths[0, 1]
    long_start, short_start = jnp.where(long_first, 0, 256), jnp.where(long_first, 768, 0)

    @pl.loop(0, 2)
    def _(document):
        body(jnp.where(document == 0, long_start, short_start), 0)

    for qi in (1, 2):
        body(long_start, qi)


def attend_kernel(tab, qkv_ref, out_ref):
    masks = head_masks()

    def body(start, qi):
        rows = pl.ds(pl.multiple_of(start + qi * BLK, BLK), BLK)
        keys = pl.ds(pl.multiple_of(start, BLK), (qi + 1) * BLK)
        q = qkv_ref[rows, 0:128] * jnp.asarray(0.125, BF16)
        k = qkv_ref[keys, 128:256]
        v = qkv_ref[keys, 256:384]
        total = None
        for m in masks:
            s = masked_scores(q * m, k, qi)
            e = jnp.exp(s - jnp.max(s, axis=1, keepdims=True))
            p = (e * (1.0 / jnp.sum(e, axis=1, keepdims=True))).astype(BF16)
            o = dot(p, v * m, NN)
            total = o if total is None else total + o
        out_ref[rows, :] = total.astype(BF16)

    for_blocks(tab, body)


def attend_call(tab, qkv):
    outs = [shape((TOK, 128), BF16)]
    return call("attend", attend_kernel, [smem(), vmem()], outs, (tab, qkv))[0]


def attend_back_kernel(tab, qkv_ref, do_ref, cos_ref, sa_ref, sb_ref, out_ref, sum_ref, dq, dk, dv):
    masks = head_masks()
    dk[...] = jnp.zeros_like(dk)
    dv[...] = jnp.zeros_like(dv)

    def body(start, qi):
        rows = pl.ds(pl.multiple_of(start + qi * BLK, BLK), BLK)
        keys = pl.ds(pl.multiple_of(start, BLK), (qi + 1) * BLK)
        q = qkv_ref[rows, 0:128]
        k = qkv_ref[keys, 128:256]
        v = qkv_ref[keys, 256:384]
        do = do_ref[rows, :]
        total = None
        for m in masks:
            qh = q * m
            doh = do * m
            s = masked_scores(qh * jnp.asarray(0.125, BF16), k, qi)
            e = jnp.exp(s - jnp.max(s, axis=1, keepdims=True))
            p = e * (1.0 / jnp.sum(e, axis=1, keepdims=True))
            dp = dot(doh, v, NT)
            delta = jnp.sum(p * dp, axis=1, keepdims=True)
            ds = (p * (dp - delta) * 0.125).astype(BF16)
            part = dot(ds, k * m, NN)
            total = part if total is None else total + part
            dk[keys, :] += dot(ds, qh, TN)
            dv[keys, :] += dot(p.astype(BF16), doh, TN)
        dq[rows, :] = total

    for_blocks(tab, body)
    for s, ref in enumerate((dq, dk, dv)):
        d = ref[...]
        if s < 2:
            d = d * cos_ref[...] - pltpu.roll(d, 128 - 16, 1) * sa_ref[...] - pltpu.roll(d, 16, 1) * sb_ref[...]
        low = d.astype(BF16)
        out_ref[:, s * 128 : (s + 1) * 128] = low
        sum_ref[:, s * 128 : (s + 1) * 128] = jnp.broadcast_to(jnp.sum(low.astype(F32), axis=0, keepdims=True), (8, 128))


def attend_back_call(tab, qkv, do, cos, sa, sb):
    outs = [shape((TOK, QKV), BF16), shape((8, QKV), F32)]
    scratch = [pltpu.VMEM((TOK, 128), F32)] * 3
    args = (tab, qkv, do, cos, sa, sb)
    return call("attend_back", attend_back_kernel, [smem()] + [vmem()] * 5, outs, args, scratch)


def project_kernel(att_ref, act_ref, *refs):
    wts, outs, whole = refs[0:2], refs[2:6], refs[6]
    place = Place()
    for half in range(2):
        spots = [[place.spot(half, j, i) for i in range(2)] for j in range(8)]

        @pl.loop(0, HALF // BLK)
        def _(t, half=half, spots=spots):
            rows = pl.ds(pl.multiple_of(half * HALF + t * BLK, BLK), BLK)
            here = pl.ds(pl.multiple_of(t * BLK, BLK), BLK)
            both = jnp.concatenate([att_ref[rows, :], act_ref[rows, :]], axis=1)
            for j in range(8):
                part = dot(both, weight_of(wts, j)[...], NT).astype(BF16)
                for i in range(2):
                    whole[spots[j][i], here, :] = part[:, i * 128 : (i + 1) * 128]

        outs[2 * half][...] = whole[0:8]
        outs[2 * half + 1][...] = whole[8:16]


def project_call(att, act, wts):
    outs = [shape((8, HALF, 128), BF16)] * 4
    scratch = [pltpu.VMEM((16, HALF, 128), BF16)]
    return call("project", project_kernel, [vmem()] * 4, outs, (att, act, *wts), scratch)


def upstream_kernel(*refs):
    place = Place()
    halves, wts, pre_ref = (refs[0:2], refs[2:4]), refs[4:6], refs[6]
    g_ref, hid_ref, att_ref, hsum_ref, gsum_ref = refs[7:12]
    mine = jnp.zeros((1, 128), F32)
    for half in range(2):
        for i, (a, k) in enumerate(PIECE_OF):
            g_ref[half * HALF : (half + 1) * HALF, pl.ds(place.lane(half, i), 128)] = halves[half][a][k]
        mine = mine + jnp.sum(halves[half][0][0].astype(F32), axis=0, keepdims=True)
    gsum_ref[...] = jnp.broadcast_to(mine, (8, 128))
    hsum_ref[...] = jnp.zeros_like(hsum_ref)

    @pl.loop(0, TOK // BLK)
    def _(t):
        rows = pl.ds(pl.multiple_of(t * BLK, BLK), BLK)
        d_act = None
        for first, n, ref in weight_blocks(wts):
            lines = slice(first * BLK, (first + n) * BLK)
            part = dot(g_ref[rows, lines], ref[...].reshape(n * BLK, ACT), NN)
            d_act = part if d_act is None else d_act + part
        att_ref[rows, :] = d_act[:, 0:128].astype(BF16)
        v = pre_ref[rows, :]
        th = gelu_tanh_part(v)
        slope = 0.5 * (1.0 + th) + 0.5 * v * (1.0 - th * th) * (0.7978845608028654 * (1.0 + 3.0 * 0.044715 * v * v))
        low = (d_act[:, 128:ACT] * slope).astype(BF16)
        hid_ref[rows, :] = low
        hsum_ref[...] += jnp.broadcast_to(jnp.sum(low.astype(F32), axis=0, keepdims=True), (8, FFL))


def upstream_call(ga, gb, wts, pre, after):
    outs = [
        shape((TOK, D), BF16),
        shape((TOK, FFL), BF16),
        shape((TOK, 128), BF16),
        shape((8, FFL), F32),
        shape((8, 128), F32),
    ]
    args = (*ga, *gb, *wts, pre)
    return call("upstream", upstream_kernel, [vmem()] * 7, outs, args, after=after)


def downstream_kernel(dm_ref, dh_ref, normed_ref, gb_ref, *refs):
    wts, outs, whole, flat = refs[0:2], refs[2:6], refs[6], refs[7]
    place = Place()
    flat[...] = jnp.zeros_like(flat)
    for half in range(2):
        spots = [[place.spot(half, j, i) for i in range(2)] for j in range(8)]

        @pl.loop(0, HALF // BLK)
        def _(b, half=half, spots=spots):
            rows = pl.ds(pl.multiple_of(half * HALF + b * BLK, BLK), BLK)
            here = pl.ds(pl.multiple_of(b * BLK, BLK), BLK)
            both = jnp.concatenate([dm_ref[rows, :], dh_ref[rows, :]], axis=1)
            s1 = jnp.zeros((BLK, 128), F32)
            s2 = jnp.zeros((BLK, 128), F32)
            for j in range(8):
                lines = slice(j * BLK, (j + 1) * BLK)
                part = dot(both, weight_of(wts, j)[...], NT)
                low = part.astype(BF16)
                u1 = part * gb_ref[0:1, lines]
                u2 = part * (normed_ref[rows, lines].astype(F32) - gb_ref[1:2, lines])
                for i in range(2):
                    cut = slice(i * 128, (i + 1) * 128)
                    whole[spots[j][i], here, :] = low[:, cut]
                    s1 = s1 + u1[:, cut]
                    s2 = s2 + u2[:, cut]
            for i in range(BLK // 128):
                cut = slice(i * 128, (i + 1) * 128)
                at = b * (BLK // 64) + 2 * i
                flat[pl.ds(at, 1), :] = jnp.sum(jnp.transpose(s1[cut, :]), axis=0, keepdims=True)
                flat[pl.ds(at + 1, 1), :] = jnp.sum(jnp.transpose(s2[cut, :]), axis=0, keepdims=True)

        low = flat[...].astype(BF16)
        for n, out in enumerate(outs[2 * half : 2 * half + 2]):
            out[:, 0:HALF, :] = whole[8 * n : 8 * n + 8]
            for c in range(8):
                out[c, HALF : HALF + PAD, :] = low


def downstream_call(dm, dh, normed, gb, wts, after):
    outs = [shape((8, HALF + PAD, 128), BF16)] * 4
    scratch = [pltpu.VMEM((16, HALF, 128), BF16), pltpu.VMEM((PAD, 128), F32)]
    args = (dm, dh, normed, gb, *wts)
    return call("downstream", downstream_kernel, [vmem()] * 6, outs, args, scratch, after)


def grad_lanes(p):
    place = lax.rem(p, 4)
    j = p + jnp.where(place == 1, 1, 0) - jnp.where(place == 2, 1, 0)
    return pl.ds(pl.multiple_of(j * BLK, BLK), BLK)


TILE = BLK + PAD
TILE_TWO = ACT + PAD
GRAD_ROWS = 7 * TILE + 2 * TILE_TWO


def grads_kernel(normed_ref, dm_ref, dh_ref, msum_ref, hsum_ref, att_ref, act_ref, g_ref, gsum_ref, keep, send, turned):
    turned[0:128, :] = jnp.transpose(att_ref[...])
    turned[128:ACT, :] = jnp.transpose(act_ref[...])
    zero = jnp.zeros((8, 128), F32)
    for first, out_ref in ((4, send), (0, keep)):

        @pl.loop(0, 4)
        def _(p, first=first, out_ref=out_ref):
            lanes = grad_lanes(first + p)
            block = normed_ref[:, lanes]
            t = 0
            for ref, sums_ref, n in ((dm_ref, msum_ref, 3), (dh_ref, hsum_ref, 4)):
                part = dot(block, ref[...], TN).astype(BF16)
                for i in range(n):
                    cut = slice(i * 128, (i + 1) * 128)
                    out_ref[p, t * TILE : t * TILE + BLK, :] = part[:, cut]
                    sums = jnp.concatenate([sums_ref[:, cut], zero], axis=0).astype(BF16)
                    out_ref[p, t * TILE + BLK : (t + 1) * TILE, :] = sums
                    t += 1
            part = dot(turned[...], g_ref[:, lanes], NN).astype(BF16)
            sums = jnp.concatenate([gsum_ref[...], zero], axis=0).astype(BF16)
            for i in range(2):
                at = 7 * TILE + i * TILE_TWO
                out_ref[p, at : at + ACT, :] = part[:, i * 128 : (i + 1) * 128]
                out_ref[p, at + ACT : at + TILE_TWO, :] = sums


def grads_call(*args, after):
    scratch = [pltpu.VMEM((ACT, TOK), BF16)]
    return call("grads", grads_kernel, [vmem()] * 9, [shape((4, GRAD_ROWS, 128), BF16)] * 2, args, scratch, after)


def fold_part(blocks, out_ref, back_ref, got, keep_out, keep_back, send):
    half = blocks // 2
    for i in range(blocks):
        for back, (ref, rows, keep) in enumerate(((out_ref, HALF, keep_out), (back_ref, HALF + PAD, keep_back))):
            if len(got) == 2:
                new = got[back][i]
            else:
                base = back * blocks * HALF + i * rows
                new = got[0][base : base + rows, :]
            total = ref[i].astype(F32) + new.astype(F32)
            if i < half:
                keep[i] = total
            else:
                at = back * half * HALF + (i - half) * rows
                send[at : at + rows, :] = total.astype(BF16)


def fold_call(blocks, a, b, *extra, after=()):
    half, n = blocks // 2, len(a)

    def kernel(*refs):
        ins, outs = refs[: 2 * n], refs[2 * n + len(extra) :]
        for h in range(2):
            mine = ins[h * n : (h + 1) * n]
            fold_part(blocks, mine[0], mine[1], mine[2:], *outs[3 * h : 3 * h + 3])
        for ref, out in zip(refs[2 * n :], outs[6:]):
            out[...] = ref[...]

    outs = [
        shape((half, HALF, 128), F32),
        shape((half, HALF + PAD, 128), F32),
        shape((half * (2 * HALF + PAD), 128), BF16),
    ] * 2 + [shape(e.shape, e.dtype) for e in extra]
    got = call("fold", kernel, [vmem()] * (2 * n + len(extra)), outs, (*a, *b, *extra), after=after)
    return got[0:3], got[3:6], got[6:]


def finish_kernel(oa, ba, ga, ob, bb, gb, x_ref, g_ref, cen_ref, inv_ref, small_ref, out_ref, grad_ref, sum_ref):
    gain = small_ref[0:1, :].astype(F32)
    shift = small_ref[2:3, :].astype(F32) + small_ref[3:4, :].astype(F32)
    total_gain = jnp.zeros((1, 128), F32)
    total_shift = jnp.zeros((1, 128), F32)
    for half, (o_ref, b_ref, got) in enumerate(((oa, ba, ga), (ob, bb, gb))):
        sums = b_ref[0, HALF : HALF + PAD, :] + got[2 * HALF : 2 * HALF + PAD, :].astype(F32)
        sums = jnp.transpose(sums) * (1.0 / D)
        for i in range(HALF // 128):
            here = slice(i * 128, (i + 1) * 128)
            there = slice(HALF + i * 128, HALF + (i + 1) * 128)
            rows = slice(half * HALF + i * 128, half * HALF + (i + 1) * 128)
            branch = o_ref[0, here, :] + got[here, :].astype(F32)
            out_ref[rows, :] = (x_ref[rows, :].astype(F32) + branch + shift).astype(BF16)
            d = b_ref[0, here, :] + got[there, :].astype(F32)
            cen = cen_ref[rows, :]
            total_gain = total_gain + jnp.sum(d * cen, axis=0, keepdims=True)
            total_shift = total_shift + jnp.sum(d, axis=0, keepdims=True)
            m1 = sums[:, 2 * i : 2 * i + 1]
            m2 = sums[:, 2 * i + 1 : 2 * i + 2]
            grad_ref[rows, :] = g_ref[rows, :].astype(F32) + inv_ref[rows, :] * (d * gain - m1 - cen * m2)
    sum_ref[...] = jnp.concatenate([total_gain, total_shift, jnp.zeros((6, 128), F32)], axis=0)


def finish_call(*args):
    outs = [shape((TOK, 128), BF16), shape((TOK, 128), F32), shape((8, 128), F32)]
    return call("finish", finish_kernel, [vmem()] * 11, outs, args, final=True)


def fold_row_call(kept, *got, parts=1, after=()):
    n = got[0].shape[0] // 2
    cut = GRAD_ROWS // parts

    def kernel(kept_ref, *refs):
        ins, keep_ref, sends = refs[: len(got)], refs[len(got)], refs[len(got) + 1 :]
        step = GRAD_ROWS // len(got)
        for i in range(n):
            for m, ref in enumerate(ins):
                rows = slice(m * step, (m + 1) * step)
                keep_ref[i, rows, :] = kept_ref[i, rows, :].astype(F32) + ref[i].astype(F32)
            for m, send in enumerate(sends):
                rows = slice(m * cut, (m + 1) * cut)
                if len(got) == 1:
                    new = ins[0][n + i, rows, :].astype(F32)
                else:
                    new = jnp.concatenate([ref[n + i].astype(F32) for ref in ins], axis=0)
                send[i] = (kept_ref[n + i, rows, :].astype(F32) + new).astype(BF16)

    outs = [shape((n, GRAD_ROWS, 128), F32)] + [shape((n, cut, 128), BF16)] * parts
    return call("fold_row", kernel, [vmem()] * (1 + len(got)), outs, (kept, *got), after=after)


def lanes_of(v, row, width):
    total = 8 * width
    return pltpu.roll(v, lax.rem(total - row * width, total), 1)[:, 0:width]


def close_kernel(kept_ref, got_ref, qkv_ref, qb_ref, up_ref, ub_ref, out_ref, down_ref, bias_ref, again_ref):
    total = lambda first, n: kept_ref[0, first : first + n, :] + got_ref[0, first : first + n, :].astype(F32)
    row = lax.axis_index("row")
    for s in range(3):
        qkv_ref[s] = total(s * TILE, BLK)
        qb_ref[s : s + 1, :] = lanes_of(total(s * TILE + BLK, PAD)[0:8], row, 16)[0:1]
    for i in range(4):
        up_ref[:, i * 128 : (i + 1) * 128] = total((3 + i) * TILE, BLK)
    bias = jnp.concatenate([total((3 + i) * TILE + BLK, PAD)[0:8] for i in range(4)], axis=1)
    ub_ref[...] = lanes_of(bias, row, 64)[0:1]
    for i in range(2):
        at = 7 * TILE + i * TILE_TWO
        out_ref[:, i * 128 : (i + 1) * 128] = total(at, 128)
        down_ref[:, i * 128 : (i + 1) * 128] = total(at + 128, FFL)
    bias = lanes_of(total(7 * TILE + ACT, PAD)[0:8], row, 16)[0:1]
    bias_ref[...] = bias
    again_ref[...] = bias


def close_call(kept, got):
    outs = [
        shape((3, BLK, 128), F32),
        shape((3, 16), F32),
        shape((BLK, FFL), F32),
        shape((1, 64), F32),
        shape((128, BLK), F32),
        shape((FFL, BLK), F32),
        shape((1, 16), F32),
        shape((1, 16), F32),
    ]
    return call("close", close_kernel, [vmem()] * 2, outs, (kept, got), final=True)


def close_norm_kernel(*refs):
    total = refs[0][...]
    for ref in refs[1:4]:
        total = total + ref[...]
    mine = lanes_of(total, lax.axis_index("row"), 16)
    refs[4][...] = mine[0:1]
    refs[5][...] = mine[1:2]


def close_norm_call(*args):
    return call("close_norm", close_norm_kernel, [vmem()] * 4, [shape((1, 16), F32)] * 2, args, final=True)


def join(*groups, after=()):
    groups = [[p if isinstance(p, tuple) else (p, 0, p.shape[0]) for p in group] for group in groups]
    flat = [p for group in groups for p in group]

    def kernel(*refs):
        ins, outs = refs[: len(flat)], refs[len(flat) :]
        n = 0
        for group, out in zip(groups, outs):
            at = 0
            for _, lo, hi in group:
                out[at : at + hi - lo] = ins[n][lo:hi]
                at += hi - lo
                n += 1

    outs = []
    for group in groups:
        first = group[0][0]
        outs.append(shape((sum(hi - lo for _, lo, hi in group),) + first.shape[1:], first.dtype))
    return call("join", kernel, [vmem()] * len(flat), outs, [p[0] for p in flat], after=after)


def fetch(copies):
    for copy in copies:
        copy.start()
    for copy in copies:
        copy.wait()


def in_hbm(*arrays):
    return [pltpu.with_memory_space_constraint(a, pltpu.HBM) for a in arrays]


def begin_kernel(x_ref, g_ref, a_ref, b_ref, sem):
    copies = []
    for half, out in enumerate((a_ref, b_ref)):
        for i, ref in enumerate((x_ref, g_ref)):
            copies.append(pltpu.make_async_copy(ref.at[pl.ds(half * HALF, HALF)], out.at[i], sem.at[half * 2 + i]))
    fetch(copies)


def begin_call(*args, after):
    scratch = [pltpu.SemaphoreType.DMA((4,))]
    specs = [pl.BlockSpec(memory_space=pltpu.HBM)] * 2
    return call("begin", begin_kernel, specs, [shape((2, HALF, 128), BF16)] * 2, in_hbm(*args), scratch, after)


def pack_kernel(qkv_ref, up_ref, out_ref, down_ref, cats, twos, out_here, down_here, sem):
    copies = [
        pltpu.make_async_copy(qkv_ref.at[s], cats.at[0, :, pl.ds(s * 128, 128)], sem.at[s]) for s in range(3)
    ]
    copies.append(pltpu.make_async_copy(up_ref, cats.at[0, :, pl.ds(QKV, FFL)], sem.at[3]))
    copies.append(pltpu.make_async_copy(out_ref, out_here, sem.at[4]))
    copies.append(pltpu.make_async_copy(down_ref, down_here, sem.at[5]))
    fetch(copies)
    twos[0, :, 0:128] = jnp.transpose(out_here[...])
    twos[0, :, 128:ACT] = jnp.transpose(down_here[...])


def pack_call(*args, after):
    outs = [shape((1, BLK, CAT), BF16), shape((1, BLK, ACT), BF16)]
    scratch = [pltpu.VMEM((128, BLK), BF16), pltpu.VMEM((FFL, BLK), BF16), pltpu.SemaphoreType.DMA((6,))]
    specs = [pl.BlockSpec(memory_space=pltpu.HBM)] * 4
    return call("pack", pack_kernel, specs, outs, in_hbm(*args), scratch, after)


def both(mine, got):
    n = mine.shape[0] // 2
    return [(mine, 0, n), (got, 0, n), (mine, n, 2 * n), (got, n, 2 * n)]


def rotary_tables(long_start):
    places = jnp.arange(TOK, dtype=jnp.int32)
    begin_second = jnp.where(long_start == 0, 768, 256)
    positions = jnp.where(places >= begin_second, places - begin_second, places)
    lane = jnp.arange(128, dtype=jnp.int32)
    spot = lane % HEAD_DIM
    half = ROT // 2
    inverse = 10000.0 ** (-2.0 * (spot % half).astype(F32) / ROT)
    angles = positions.astype(F32)[:, None] * inverse[None, :]
    turned = (spot < ROT)[None, :]
    cos = jnp.where(turned, jnp.cos(angles), 1.0)
    sine = jnp.sin(angles)
    low = jnp.where((spot < half)[None, :], -sine, 0.0)
    high = jnp.where(((spot >= half) & (spot < ROT))[None, :], sine, 0.0)
    return cos, low, high


def shards(x, lengths, w_qkv, b_qkv, w_out, b_out, w_up, b_up, w_down, b_down, gain, shift, g):
    row = lax.axis_index("row")
    cos, sa, sb = rotary_tables(jnp.where(lengths[0, 0] > lengths[0, 1], 0, 256))

    def spread(v, width):
        wide = jnp.zeros(v.shape[:-1] + (8, width), BF16)
        return lax.dynamic_update_slice_in_dim(wide, v[..., None, :], row, v.ndim - 1).reshape(-1, 128)

    small = [spread(jnp.stack([gain, shift, b_out, b_down]), 16), spread(b_qkv, 16), spread(b_up, 64)]
    small = jnp.concatenate(small + [jnp.zeros((PAD - 11, 128), BF16)])
    a, b = begin_call(x, g, after=(small,))
    a_got, b_got = exchange(a, "x", 0), exchange(b, "y", 0)
    small = small + exchange(small, "c")
    cats, twos = pack_call(w_qkv.transpose(1, 0, 2), w_up, w_out, w_down, after=(small,))
    small = small + exchange(small, "z", 0)
    small, cats, twos, a, b = join([small], [cats], [twos], both(a, a_got), both(b, b_got))
    a_got, b_got = exchange(a, "x", 1), exchange(b, "y", 1)
    cats_got, twos_got = exchange(cats, "z", 0), exchange(twos, "z", 0)
    small = small + exchange(small, "z", 1)
    tiny = small[None]
    tiny_got = exchange(tiny, "x", 0)
    tiny, cats, a, b = join([tiny, tiny_got], [cats, cats_got], both(a, a_got), both(b, b_got), after=(twos_got,))
    tiny_got = exchange(tiny, "x", 1)
    a_got, b_got = exchange(a, "y", 0), exchange(b, "x", 0)
    cats_got = exchange(cats, "z", 1)
    (tiny,) = join([tiny, tiny_got])
    tiny_got = exchange(tiny, "y", 1)
    first = lambda v, got: [(v, 0, 4), (got, 0, 4)]
    last = lambda v, got: [(v, 4, 8), (got, 4, 8)]
    tiny, xa, xb, cats, twos, ga, gb = join(
        [tiny, tiny_got],
        first(a, a_got),
        first(b, b_got),
        [cats, cats_got],
        [twos, twos_got],
        last(a, a_got),
        last(b, b_got),
    )
    tiny = (tiny, exchange(tiny, "y", 0))
    xa, xb = (xa, exchange(xa, "y", 1)), (xb, exchange(xb, "x", 1))
    cats = (cats, exchange(cats, "c"))
    twos_got = exchange(twos, "z", 1)
    ga, gb = (ga, exchange(ga, "y", 1)), (gb, exchange(gb, "x", 1))
    (twos,) = join([twos, twos_got])
    twos = (twos, exchange(twos, "c"))

    normed, qkv, pre, act, centered, inv, gains = norm_call(xa, xb, tiny, cats, cos, sa, sb)
    att = attend_call(lengths, qkv)
    out_a, send_a, out_b, send_b = project_call(att, act, twos)
    out_a_got, out_b_got = exchange(send_a, "y", 0), exchange(send_b, "x", 0)
    g_all, d_hid, d_att, hsum, gsum = upstream_call(ga, gb, twos, pre, (out_a,))
    d_mix, msum = attend_back_call(lengths, qkv, d_att, cos, sa, sb)
    back_a, send_a, back_b, send_b = downstream_call(d_mix, d_hid, normed, gains, cats, (out_a_got, out_b_got))
    back_a_got, back_b_got = exchange(send_a, "y", 0), exchange(send_b, "x", 0)
    keep, send = grads_call(normed, d_mix, d_hid, msum, hsum, att, act, g_all, gsum, after=(back_a,))
    a, b, (send,) = fold_call(8, (out_a, back_a, out_a_got, back_a_got), (out_b, back_b, out_b_got, back_b_got), send)
    a_got, b_got = exchange(a[2], "y", 1), exchange(b[2], "x", 1)
    keep, *sends = fold_row_call(keep, exchange(send, "c"), parts=3)
    got = [exchange(send, "z", 0) for send in sends]
    a, b, _ = fold_call(4, (a[0], a[1], a_got), (b[0], b[1], b_got), after=(got[0],))
    a_got, b_got = exchange(a[2], "x", 0), exchange(b[2], "y", 0)
    a, b, _ = fold_call(2, (a[0], a[1], a_got), (b[0], b[1], b_got), after=(got[1],))
    a_got, b_got = exchange(a[2], "x", 1), exchange(b[2], "y", 1)
    keep, send = fold_row_call(keep, *got, after=(a[0],))
    got = exchange(send, "z", 1)
    block_out, input_grad, sums = finish_call(a[0], a[1], a_got, b[0], b[1], b_got, x, g, centered, inv, small)
    sums = sums + exchange(sums, "c")
    gain_grad, shift_grad = close_norm_call(sums, *(exchange(sums, "z", n) for n in range(3)))
    qkv_grad, qkv_bias, up_grad, up_bias, out_grad, down_grad, out_bias, down_bias = close_call(keep, got)
    return (
        block_out,
        input_grad,
        qkv_grad.transpose(1, 0, 2),
        qkv_bias,
        out_grad,
        out_bias.reshape(16),
        up_grad,
        up_bias.reshape(64),
        down_grad,
        down_bias.reshape(16),
        gain_grad.reshape(16),
        shift_grad.reshape(16),
    )


def solution(mesh):
    both = P(("col", "row"))
    in_specs = (
        P("row", "col"),
        P("row", None),
        P("row", None, "col"),
        P(None, ("col", "row")),
        P("col", "row"),
        both,
        P("row", "col"),
        both,
        P("col", "row"),
        both,
        both,
        both,
        P("row", "col"),
    )
    out_specs = (
        P("row", "col"),
        P("row", "col"),
        P("row", None, "col"),
        P(None, ("col", "row")),
        P("col", "row"),
        both,
        P("row", "col"),
        both,
        P("col", "row"),
        both,
        both,
        both,
    )
    return jax.shard_map(shards, mesh=mesh, in_specs=in_specs, out_specs=out_specs, check_vma=False)
```

profile of v0, /device:TPU:1, one launch (start us, length us, event | category | flops | bytes accessed | tf_op | source)
XLA Modules:
  0.0 175.4 jit_solution(6128679888665522026)
XLA Ops:
  4.4 3.4 %collective-permute-start.2 = (bf16[2,512,128]{2,1,0:T(8,128)(2,1)S(1)}, bf16[2,512,128]{2,1,0:T(8,128)(2,1)S(1)}, u32[]{:S(2)}, u32[]{:S(2)}) collective-permute-start(bf16[2,512,128]{2,1,0:T(8,128)(2,1)S(1)} %get-tuple-element.96.refs_3_.refs_5_), channel_id=1, source_target_pairs={{0,1},{1,0},{2,3},{3,2},{4,5},{5,4},{6,7},{7,6},{8,9},{9,8},{10,11... | collective-permute-start | bytes 786440 | tf_op jit(solution)/shard_map/ppermute | solution.py:44
  7.8 2.7 %collective-permute-start.3 = (bf16[2,512,128]{2,1,0:T(8,128)(2,1)S(1)}, bf16[2,512,128]{2,1,0:T(8,128)(2,1)S(1)}, u32[]{:S(2)}, u32[]{:S(2)}) collective-permute-start(bf16[2,512,128]{2,1,0:T(8,128)(2,1)S(1)} %get-tuple-element.97.refs_7_.refs_9_), channel_id=1, source_target_pairs={{0,4},{1,5},{2,6},{3,7},{4,0},{5,1},{6,2},{7,3},{8,12},{9,13},{10,... | collective-permute-start | bytes 786440 | tf_op jit(solution)/shard_map/ppermute | solution.py:44
  11.7 3.8 %collective-permute-start.1 = (bf16[16,128]{1,0:T(8,128)(2,1)S(1)}, bf16[16,128]{1,0:T(8,128)(2,1)S(1)}, u32[]{:S(2)}, u32[]{:S(2)}) collective-permute-start(bf16[16,128]{1,0:T(8,128)(2,1)S(1)} %fusion.8.refs_4_), channel_id=1, source_target_pairs={{0,32},{1,33},{2,34},{3,35},{4,36},{5,37},{6,38},{7,39},{8,40},{9,... | collective-permute-start | bytes 12296 | tf_op jit(solution)/shard_map/ppermute | solution.py:44
  20.0 2.8 %collective-permute-done.4 = bf16[16,128]{1,0:T(8,128)(2,1)S(1)} collective-permute-done((bf16[16,128]{1,0:T(8,128)(2,1)S(1)}, bf16[16,128]{1,0:T(8,128)(2,1)S(1)}, u32[]{:S(2)}, u32[]{:S(2)}) %collective-permute-start.4) | collective-permute-done | bytes 4128 | tf_op jit(solution)/shard_map/ppermute | solution.py:44
  23.7 2.8 %collective-permute-done.5.refs_1_ = bf16[1,16,128]{2,1,0:T(8,128)(2,1)S(1)} collective-permute-done((bf16[1,16,128]{2,1,0:T(8,128)(2,1)S(1)}, bf16[1,16,128]{2,1,0:T(8,128)(2,1)S(1)}, u32[]{:S(2)}, u32[]{:S(2)}) %collective-permute-start.5) | collective-permute-done | bytes 4128 | tf_op jit(solution)/shard_map/ppermute | solution.py:44
  26.5 2.9 %collective-permute-done.9.refs_12_.refs_9_ = bf16[1,256,640]{2,1,0:T(8,128)(2,1)S(1)} collective-permute-done((bf16[1,256,640]{2,1,0:T(8,128)(2,1)S(1)}, bf16[1,256,640]{2,1,0:T(8,128)(2,1)S(1)}, u32[]{:S(2)}, u32[]{:S(2)}) %collective-permute-start.9) | collective-permute-done | bytes 327712 | tf_op jit(solution)/shard_map/ppermute | solution.py:44
  33.4 2.9 %collective-permute-done.10.refs_1_ = bf16[2,16,128]{2,1,0:T(8,128)(2,1)S(1)} collective-permute-done((bf16[2,16,128]{2,1,0:T(8,128)(2,1)S(1)}, bf16[2,16,128]{2,1,0:T(8,128)(2,1)S(1)}, u32[]{:S(2)}, u32[]{:S(2)}) %collective-permute-start.10) | collective-permute-done | bytes 8224 | tf_op jit(solution)/shard_map/ppermute | solution.py:44
  36.3 3.1 %collective-permute-done.11.refs_1_ = bf16[4,16,128]{2,1,0:T(8,128)(2,1)S(1)} collective-permute-done((bf16[4,16,128]{2,1,0:T(8,128)(2,1)S(1)}, bf16[4,16,128]{2,1,0:T(8,128)(2,1)S(1)}, u32[]{:S(2)}, u32[]{:S(2)}) %collective-permute-start.11) | collective-permute-done | bytes 16416 | tf_op jit(solution)/shard_map/ppermute | solution.py:44
  39.4 6.5 %collective-permute-done.14.refs_7_ = bf16[2,256,896]{2,1,0:T(8,128)(2,1)S(1)} collective-permute-done((bf16[2,256,896]{2,1,0:T(8,128)(2,1)S(1)}, bf16[2,256,896]{2,1,0:T(8,128)(2,1)S(1)}, u32[]{:S(2)}, u32[]{:S(2)}) %collective-permute-start.14) | collective-permute-done | bytes 917536 | tf_op jit(solution)/shard_map/ppermute | solution.py:44
  50.9 7.0 %collective-permute-done.19.refs_1_ = bf16[2,256,640]{2,1,0:T(8,128)(2,1)S(1)} collective-permute-done((bf16[2,256,640]{2,1,0:T(8,128)(2,1)S(1)}, bf16[2,256,640]{2,1,0:T(8,128)(2,1)S(1)}, u32[]{:S(2)}, u32[]{:S(2)}) %collective-permute-start.19) | collective-permute-done | bytes 655392 | tf_op jit(solution)/shard_map/ppermute | solution.py:44
  68.5 9.3 %norm_proj.1 = (bf16[1024,2048]{1,0:T(8,128)(2,1)S(1)}, bf16[1024,384]{1,0:T(8,128)(2,1)S(1)}, f32[1024,512]{1,0:T(8,128)S(1)}, bf16[1024,512]{1,0:T(8,128)(2,1)...) custom-call(bf16[8,512,128]{2,1,0:T(8,128)(2,1)S(1)} %get-tuple-element.107.refs_0_, ...), custom_call_target="tpu_custom_call" | custom-call | flops 2249999872 | tf_op jit(solution)/shard_map/norm_proj/pallas_call | solution.py:132
  77.8 3.2 %attend.1.att_ref.refs_5_ = bf16[1024,128]{1,0:T(8,128)(2,1)S(1)} custom-call(s32[1,2]{1,0:T(1,128)S(1)} %copy-done.2, bf16[1024,384]{1,0:T(8,128)(2,1)S(1)} %get-tuple-element.111.qkv_ref), custom_call_target="tpu_custom_call" | custom-call | flops 750000000 | tf_op jit(solution)/shard_map/attend/pallas_call | solution.py:132
  81.0 4.6 %project.1 = (bf16[8,512,128]{2,1,0:T(8,128)(2,1)S(1)}, bf16[8,512,128]{2,1,0:T(8,128)(2,1)S(1)}, bf16[8,512,128]{2,1,0:T(8,128)(2,1)S(1)}, bf16[8,512,128]{2,1,0:T(8,128)(2,1)S(1)}) custom-call(bf16[1024,128]{1,0:T(8,128)(2,1)S(1)} %attend.1.att_ref.refs_5_, bf16[1024,512]{1,0:T(8,128)(2,1)S(1)} %get-tuple-element.112.act_ref.refs_6_, ...), custom_call_target="tpu_custom_call" | custom-call | flops 1250000000 | tf_op jit(solution)/shard_map/project/pallas_call | solution.py:132
  88.3 5.9 %upstream.1 = (bf16[1024,2048]{1,0:T(8,128)(2,1)S(1)}, bf16[1024,512]{1,0:T(8,128)(2,1)S(1)}, bf16[1024,128]{1,0:T(8,128)(2,1)S(1)}, f32[8,512]{1,0:T(8,128)S(1)}, f32[8,128]{1,0:T(8,128)S(1)}) custom-call(bf16[8,512,128]{2,1,0:T(8,128)(2,1)S(1)} %get-tuple-element.115.refs_0_, bf16[8,512,128]{2,1,0:T(8,128)(2,1)S(1)} %collective-permute-done.21.refs_1_, ...), custom_call_target="tpu_custom_call" | custom-call | flops 1500000000 | tf_op jit(solution)/shard_map/upstream/pallas_call | solution.py:132
  94.3 7.2 %attend_back.1 = (bf16[1024,384]{1,0:T(8,128)(2,1)S(1)}, f32[8,384]{1,0:T(8,128)S(1)}) custom-call(s32[1,2]{1,0:T(1,128)S(1)} %copy-done.2, bf16[1024,384]{1,0:T(8,128)(2,1)S(1)} %get-tuple-element.111.qkv_ref, bf16[1024,128]{1,0:T(8,128)(2,1)S(1)} %get-tuple-element.118.do_ref, f32[1024,128]{1,0:T(8,128)S(1)} %get-tuple-element.178.refs_8_.cos_ref, ...), custom_call_target="tpu_custom_call" | custom-call | flops 1750000000 | tf_op jit(solution)/shard_map/attend_back/pallas_call | solution.py:132
  101.4 6.5 %downstream.1 = (bf16[8,528,128]{2,1,0:T(8,128)(2,1)S(1)}, bf16[8,528,128]{2,1,0:T(8,128)(2,1)S(1)}, bf16[8,528,128]{2,1,0:T(8,128)(2,1)S(1)}, bf16[8,528,128]{2,1,0:T(8,128)(2,1)S(1)}) custom-call(bf16[1024,384]{1,0:T(8,128)(2,1)S(1)} %get-tuple-element.119.refs_0_.refs_1_, bf16[1024,512]{1,0:T(8,128)(2,1)S(1)} %get-tuple-element.120.refs_1_.refs_2_, ...), custom_call_target="tpu_custom_call" | custom-call | flops 1500000000 | tf_op jit(solution)/shard_map/downstream/pallas_call | solution.py:132
  110.8 9.2 %grads.1 = (bf16[4,3216,128]{2,1,0:T(8,128)(2,1)S(1)}, bf16[4,3216,128]{2,1,0:T(8,128)(2,1)S(1)}) custom-call(bf16[1024,2048]{1,0:T(8,128)(2,1)S(1)} %get-tuple-element.121.refs_2_.refs_0_, bf16[1024,384]{1,0:T(8,128)(2,1)S(1)} %get-tuple-element.119.refs_0_.refs_1_, bf16[1024,512]{1,0:T(8,128)(2,1)S(1)} %get-tuple-element.120.refs_1_.refs_2_, ...), custom_call_target="tpu_custom_call" | custom-call | flops 2750000128 | tf_op jit(solution)/shard_map/grads/pallas_call | solution.py:132
  120.0 3.2 %collective-permute-done.25.refs_3_ = bf16[8,528,128]{2,1,0:T(8,128)(2,1)S(1)} collective-permute-done((bf16[8,528,128]{2,1,0:T(8,128)(2,1)S(1)}, bf16[8,528,128]{2,1,0:T(8,128)(2,1)S(1)}, u32[]{:S(2)}, u32[]{:S(2)}) %collective-permute-start.25) | collective-permute-done | bytes 1081376 | tf_op jit(solution)/shard_map/ppermute | solution.py:44
  127.7 4.3 %collective-permute-done.29.refs_0_ = bf16[4,3216,128]{2,1,0:T(8,128)(2,1)S(1)} collective-permute-done((bf16[4,3216,128]{2,1,0:T(8,128)(2,1)S(1)}, bf16[4,3216,128]{2,1,0:T(8,128)(2,1)S(1)}, u32[]{:S(2)}, u32[]{:S(2)}) %collective-permute-start.29) | collective-permute-done | bytes 3293216 | tf_op jit(solution)/shard_map/ppermute | solution.py:44
  137.7 2.6 %collective-permute-done.27.refs_2_ = bf16[4160,128]{1,0:T(8,128)(2,1)S(1)} collective-permute-done((bf16[4160,128]{1,0:T(8,128)(2,1)S(1)}, bf16[4160,128]{1,0:T(8,128)(2,1)S(1)}, u32[]{:S(2)}, u32[]{:S(2)}) %collective-permute-start.27) | collective-permute-done | bytes 1064992 | tf_op jit(solution)/shard_map/ppermute | solution.py:44
  148.1 4.2 %collective-permute-done.31.refs_2_ = bf16[2080,128]{1,0:T(8,128)(2,1)S(1)} collective-permute-done((bf16[2080,128]{1,0:T(8,128)(2,1)S(1)}, bf16[2080,128]{1,0:T(8,128)(2,1)S(1)}, u32[]{:S(2)}, u32[]{:S(2)}) %collective-permute-start.31) | collective-permute-done | bytes 532512 | tf_op jit(solution)/shard_map/ppermute | solution.py:44
  156.0 4.0 %collective-permute-done.34.ga = bf16[1040,128]{1,0:T(8,128)(2,1)S(1)} collective-permute-done((bf16[1040,128]{1,0:T(8,128)(2,1)S(1)}, bf16[1040,128]{1,0:T(8,128)(2,1)S(1)}, u32[]{:S(2)}, u32[]{:S(2)}) %collective-permute-start.34) | collective-permute-done | bytes 266272 | tf_op jit(solution)/shard_map/ppermute | solution.py:44
  162.0 6.5 %collective-permute-start.38 = (f32[8,128]{1,0:T(8,128)S(1)}, f32[8,128]{1,0:T(8,128)S(1)}, u32[]{:S(2)}, u32[]{:S(2)}) collective-permute-start(f32[8,128]{1,0:T(8,128)S(1)} %get-tuple-element.173), channel_id=1, source_target_pairs={{0,16},{1,17},{2,18},{3,19},{4,20},{5,21},{6,22},{7,23},{8,24},{9,... | collective-permute-start | bytes 12296 | tf_op jit(solution)/shard_map/ppermute | solution.py:44
  169.8 2.8 %collective-permute-start.39 = (f32[8,128]{1,0:T(8,128)S(1)}, f32[8,128]{1,0:T(8,128)S(1)}, u32[]{:S(2)}, u32[]{:S(2)}) collective-permute-start(f32[8,128]{1,0:T(8,128)S(1)} %add.56.refs_0_), channel_id=1, source_target_pairs={{0,32},{1,33},{2,34},{3,35},{4,36},{5,37},{6,38},{7,39},{8,40},{9,... | collective-permute-start | bytes 12296 | tf_op jit(solution)/shard_map/ppermute | solution.py:44
  (113 shorter events, 61.7 us)
Async XLA Ops:
  4.4 12.5 %collective-permute-start.2 = (bf16[2,512,128]{2,1,0:T(8,128)(2,1)S(1)}, bf16[2,512,128]{2,1,0:T(8,128)(2,1)S(1)}, u32[]{:S(2)}, u32[]{:S(2)}) collective-permute-start(bf16[2,512,128]{2,1,0:T(8,128)(2,1)S(1)} %get-tuple-element.96.refs_3_.refs_5_), channel_id=1, source_target_pairs={{0,1},{1,0},{2,3},{3,2},{4,5},{5,4},{6,7},{7,6},{8,9},{9,8},{10,11... | collective-permute-start | bytes 786440 | tf_op jit(solution)/shard_map/ppermute | solution.py:44
  17.1 12.4 %collective-permute-start.7 = (bf16[4,512,128]{2,1,0:T(8,128)(2,1)S(1)}, bf16[4,512,128]{2,1,0:T(8,128)(2,1)S(1)}, u32[]{:S(2)}, u32[]{:S(2)}) collective-permute-start(bf16[4,512,128]{2,1,0:T(8,128)(2,1)S(1)} %get-tuple-element.100.refs_4_.refs_6_), channel_id=1, source_target_pairs={{0,3},{1,2},{2,1},{3,0},{4,7},{5,6},{6,5},{7,4},{8,11},{9,10},{10,... | collective-permute-start | bytes 1572872 | tf_op jit(solution)/shard_map/ppermute | solution.py:44
  17.2 12.3 %collective-permute-start.8 = (bf16[4,512,128]{2,1,0:T(8,128)(2,1)S(1)}, bf16[4,512,128]{2,1,0:T(8,128)(2,1)S(1)}, u32[]{:S(2)}, u32[]{:S(2)}) collective-permute-start(bf16[4,512,128]{2,1,0:T(8,128)(2,1)S(1)} %get-tuple-element.101.refs_8_.refs_10_), channel_id=1, source_target_pairs={{0,12},{1,13},{2,14},{3,15},{4,8},{5,9},{6,10},{7,11},{8,4},{9,5},... | collective-permute-start | bytes 1572872 | tf_op jit(solution)/shard_map/ppermute | solution.py:44
  17.3 12.2 %collective-permute-start.6 = (bf16[1,256,896]{2,1,0:T(8,128)(2,1)S(1)}, bf16[1,256,896]{2,1,0:T(8,128)(2,1)S(1)}, u32[]{:S(2)}, u32[]{:S(2)}) collective-permute-start(bf16[1,256,896]{2,1,0:T(8,128)(2,1)S(1)} %get-tuple-element.99.refs_2_), channel_id=1, source_target_pairs={{0,32},{1,33},{2,34},{3,35},{4,36},{5,37},{6,38},{7,39},{8,40},{9,... | collective-permute-start | bytes 1376264 | tf_op jit(solution)/shard_map/ppermute | solution.py:44
  19.6 9.8 %collective-permute-start.9 = (bf16[1,256,640]{2,1,0:T(8,128)(2,1)S(1)}, bf16[1,256,640]{2,1,0:T(8,128)(2,1)S(1)}, u32[]{:S(2)}, u32[]{:S(2)}) collective-permute-start(bf16[1,256,640]{2,1,0:T(8,128)(2,1)S(1)} %get-tuple-element.102.refs_8_), channel_id=1, source_target_pairs={{0,32},{1,33},{2,34},{3,35},{4,36},{5,37},{6,38},{7,39},{8,40},{9,... | collective-permute-start | bytes 983048 | tf_op jit(solution)/shard_map/ppermute | solution.py:44
  29.7 16.3 %collective-permute-start.12 = (bf16[8,512,128]{2,1,0:T(8,128)(2,1)S(1)}, bf16[8,512,128]{2,1,0:T(8,128)(2,1)S(1)}, u32[]{:S(2)}, u32[]{:S(2)}) collective-permute-start(bf16[8,512,128]{2,1,0:T(8,128)(2,1)S(1)} %get-tuple-element.104.refs_2_.refs_10_), channel_id=1, source_target_pairs={{0,4},{1,5},{2,6},{3,7},{4,0},{5,1},{6,2},{7,3},{8,12},{9,13},{10,... | collective-permute-start | bytes 3145736 | tf_op jit(solution)/shard_map/ppermute | solution.py:44
  30.9 15.2 %collective-permute-start.13 = (bf16[8,512,128]{2,1,0:T(8,128)(2,1)S(1)}, bf16[8,512,128]{2,1,0:T(8,128)(2,1)S(1)}, u32[]{:S(2)}, u32[]{:S(2)}) collective-permute-start(bf16[8,512,128]{2,1,0:T(8,128)(2,1)S(1)} %get-tuple-element.105.refs_4_.refs_12_), channel_id=1, source_target_pairs={{0,1},{1,0},{2,3},{3,2},{4,5},{5,4},{6,7},{7,6},{8,9},{9,8},{10,11... | collective-permute-start | bytes 3145736 | tf_op jit(solution)/shard_map/ppermute | solution.py:44
  33.4 12.5 %collective-permute-start.14 = (bf16[2,256,896]{2,1,0:T(8,128)(2,1)S(1)}, bf16[2,256,896]{2,1,0:T(8,128)(2,1)S(1)}, u32[]{:S(2)}, u32[]{:S(2)}) collective-permute-start(bf16[2,256,896]{2,1,0:T(8,128)(2,1)S(1)} %get-tuple-element.106.refs_6_), channel_id=1, source_target_pairs={{0,96},{1,97},{2,98},{3,99},{4,100},{5,101},{6,102},{7,103},{8,104... | collective-permute-start | bytes 2752520 | tf_op jit(solution)/shard_map/ppermute | solution.py:44
  46.6 21.9 %collective-permute-start.18 = (bf16[4,256,896]{2,1,0:T(8,128)(2,1)S(1)}, bf16[4,256,896]{2,1,0:T(8,128)(2,1)S(1)}, u32[]{:S(2)}, u32[]{:S(2)}) collective-permute-start(bf16[4,256,896]{2,1,0:T(8,128)(2,1)S(1)} %get-tuple-element.110.refs_6_.refs_4_), channel_id=1, source_target_pairs={{0,16},{1,17},{2,18},{3,19},{4,20},{5,21},{6,22},{7,23},{8,24},{9,... | collective-permute-start | bytes 5505032 | tf_op jit(solution)/shard_map/ppermute | solution.py:44
  48.7 18.6 %collective-permute-start.15 = (bf16[8,512,128]{2,1,0:T(8,128)(2,1)S(1)}, bf16[8,512,128]{2,1,0:T(8,128)(2,1)S(1)}, u32[]{:S(2)}, u32[]{:S(2)}) collective-permute-start(bf16[8,512,128]{2,1,0:T(8,128)(2,1)S(1)} %get-tuple-element.107.refs_0_), channel_id=1, source_target_pairs={{0,12},{1,13},{2,14},{3,15},{4,8},{5,9},{6,10},{7,11},{8,4},{9,5},... | collective-permute-start | bytes 3145736 | tf_op jit(solution)/shard_map/ppermute | solution.py:44
  50.2 18.3 %collective-permute-start.16 = (bf16[8,512,128]{2,1,0:T(8,128)(2,1)S(1)}, bf16[8,512,128]{2,1,0:T(8,128)(2,1)S(1)}, u32[]{:S(2)}, u32[]{:S(2)}) collective-permute-start(bf16[8,512,128]{2,1,0:T(8,128)(2,1)S(1)} %get-tuple-element.108.refs_2_), channel_id=1, source_target_pairs={{0,3},{1,2},{2,1},{3,0},{4,7},{5,6},{6,5},{7,4},{8,11},{9,10},{10,... | collective-permute-start | bytes 3145736 | tf_op jit(solution)/shard_map/ppermute | solution.py:44
  58.0 23.0 %collective-permute-start.20 = (bf16[4,256,640]{2,1,0:T(8,128)(2,1)S(1)}, bf16[4,256,640]{2,1,0:T(8,128)(2,1)S(1)}, u32[]{:S(2)}, u32[]{:S(2)}) collective-permute-start(bf16[4,256,640]{2,1,0:T(8,128)(2,1)S(1)} %join.9.refs_0_.refs_4_), channel_id=1, source_target_pairs={{0,16},{1,17},{2,18},{3,19},{4,20},{5,21},{6,22},{7,23},{8,24},{9,... | collective-permute-start | bytes 3932168 | tf_op jit(solution)/shard_map/ppermute | solution.py:44
  67.0 21.4 %collective-permute-start.21 = (bf16[8,512,128]{2,1,0:T(8,128)(2,1)S(1)}, bf16[8,512,128]{2,1,0:T(8,128)(2,1)S(1)}, u32[]{:S(2)}, u32[]{:S(2)}) collective-permute-start(bf16[8,512,128]{2,1,0:T(8,128)(2,1)S(1)} %get-tuple-element.115.refs_0_), channel_id=1, source_target_pairs={{0,12},{1,13},{2,14},{3,15},{4,8},{5,9},{6,10},{7,11},{8,4},{9,5},... | collective-permute-start | bytes 3145736 | tf_op jit(solution)/shard_map/ppermute | solution.py:44
  67.3 21.0 %collective-permute-start.22 = (bf16[8,512,128]{2,1,0:T(8,128)(2,1)S(1)}, bf16[8,512,128]{2,1,0:T(8,128)(2,1)S(1)}, u32[]{:S(2)}, u32[]{:S(2)}) collective-permute-start(bf16[8,512,128]{2,1,0:T(8,128)(2,1)S(1)} %get-tuple-element.116.refs_2_), channel_id=1, source_target_pairs={{0,3},{1,2},{2,1},{3,0},{4,7},{5,6},{6,5},{7,4},{8,11},{9,10},{10,... | collective-permute-start | bytes 3145736 | tf_op jit(solution)/shard_map/ppermute | solution.py:44
  85.7 15.8 %collective-permute-start.23 = (bf16[8,512,128]{2,1,0:T(8,128)(2,1)S(1)}, bf16[8,512,128]{2,1,0:T(8,128)(2,1)S(1)}, u32[]{:S(2)}, u32[]{:S(2)}) collective-permute-start(bf16[8,512,128]{2,1,0:T(8,128)(2,1)S(1)} %get-tuple-element.123), channel_id=1, source_target_pairs={{0,4},{1,5},{2,6},{3,7},{4,0},{5,1},{6,2},{7,3},{8,12},{9,13},{10,... | collective-permute-start | bytes 3145736 | tf_op jit(solution)/shard_map/ppermute | solution.py:44
  86.4 15.1 %collective-permute-start.24 = (bf16[8,512,128]{2,1,0:T(8,128)(2,1)S(1)}, bf16[8,512,128]{2,1,0:T(8,128)(2,1)S(1)}, u32[]{:S(2)}, u32[]{:S(2)}) collective-permute-start(bf16[8,512,128]{2,1,0:T(8,128)(2,1)S(1)} %get-tuple-element.124), channel_id=1, source_target_pairs={{0,1},{1,0},{2,3},{3,2},{4,5},{5,4},{6,7},{7,6},{8,9},{9,8},{10,11... | collective-permute-start | bytes 3145736 | tf_op jit(solution)/shard_map/ppermute | solution.py:44
  107.9 15.3 %collective-permute-start.25 = (bf16[8,528,128]{2,1,0:T(8,128)(2,1)S(1)}, bf16[8,528,128]{2,1,0:T(8,128)(2,1)S(1)}, u32[]{:S(2)}, u32[]{:S(2)}) collective-permute-start(bf16[8,528,128]{2,1,0:T(8,128)(2,1)S(1)} %get-tuple-element.126), channel_id=1, source_target_pairs={{0,4},{1,5},{2,6},{3,7},{4,0},{5,1},{6,2},{7,3},{8,12},{9,13},{10,... | collective-permute-start | bytes 3244040 | tf_op jit(solution)/shard_map/ppermute | solution.py:44
  109.7 15.2 %collective-permute-start.26 = (bf16[8,528,128]{2,1,0:T(8,128)(2,1)S(1)}, bf16[8,528,128]{2,1,0:T(8,128)(2,1)S(1)}, u32[]{:S(2)}, u32[]{:S(2)}) collective-permute-start(bf16[8,528,128]{2,1,0:T(8,128)(2,1)S(1)} %get-tuple-element.129), channel_id=1, source_target_pairs={{0,1},{1,0},{2,3},{3,2},{4,5},{5,4},{6,7},{7,6},{8,9},{9,8},{10,11... | collective-permute-start | bytes 3244040 | tf_op jit(solution)/shard_map/ppermute | solution.py:44
  126.1 14.2 %collective-permute-start.27 = (bf16[4160,128]{1,0:T(8,128)(2,1)S(1)}, bf16[4160,128]{1,0:T(8,128)(2,1)S(1)}, u32[]{:S(2)}, u32[]{:S(2)}) collective-permute-start(bf16[4160,128]{1,0:T(8,128)(2,1)S(1)} %get-tuple-element.137), channel_id=1, source_target_pairs={{0,12},{1,13},{2,14},{3,15},{4,8},{5,9},{6,10},{7,11},{8,4},{9,5},... | collective-permute-start | bytes 3194888 | tf_op jit(solution)/shard_map/ppermute | solution.py:44
  126.7 14.1 %collective-permute-start.28 = (bf16[4160,128]{1,0:T(8,128)(2,1)S(1)}, bf16[4160,128]{1,0:T(8,128)(2,1)S(1)}, u32[]{:S(2)}, u32[]{:S(2)}) collective-permute-start(bf16[4160,128]{1,0:T(8,128)(2,1)S(1)} %get-tuple-element.140), channel_id=1, source_target_pairs={{0,3},{1,2},{2,1},{3,0},{4,7},{5,6},{6,5},{7,4},{8,11},{9,10},{10,... | collective-permute-start | bytes 3194888 | tf_op jit(solution)/shard_map/ppermute | solution.py:44
  132.6 9.9 %collective-permute-start.30 = (bf16[2,1072,128]{2,1,0:T(8,128)(2,1)S(1)}, bf16[2,1072,128]{2,1,0:T(8,128)(2,1)S(1)}, u32[]{:S(2)}, u32[]{:S(2)}) collective-permute-start(bf16[2,1072,128]{2,1,0:T(8,128)(2,1)S(1)} %get-tuple-element.143), channel_id=1, source_target_pairs={{0,32},{1,33},{2,34},{3,35},{4,36},{5,37},{6,38},{7,39},{8,40},{9,... | collective-permute-start | bytes 1646600 | tf_op jit(solution)/shard_map/ppermute | solution.py:44
  135.0 13.1 %collective-permute-start.33 = (bf16[2,1072,128]{2,1,0:T(8,128)(2,1)S(1)}, bf16[2,1072,128]{2,1,0:T(8,128)(2,1)S(1)}, u32[]{:S(2)}, u32[]{:S(2)}) collective-permute-start(bf16[2,1072,128]{2,1,0:T(8,128)(2,1)S(1)} %get-tuple-element.150), channel_id=1, source_target_pairs={{0,32},{1,33},{2,34},{3,35},{4,36},{5,37},{6,38},{7,39},{8,40},{9,... | collective-permute-start | bytes 1646600 | tf_op jit(solution)/shard_map/ppermute | solution.py:44
  135.4 18.6 %collective-permute-start.36 = (bf16[2,1072,128]{2,1,0:T(8,128)(2,1)S(1)}, bf16[2,1072,128]{2,1,0:T(8,128)(2,1)S(1)}, u32[]{:S(2)}, u32[]{:S(2)}) collective-permute-start(bf16[2,1072,128]{2,1,0:T(8,128)(2,1)S(1)} %get-tuple-element.162), channel_id=1, source_target_pairs={{0,32},{1,33},{2,34},{3,35},{4,36},{5,37},{6,38},{7,39},{8,40},{9,... | collective-permute-start | bytes 1646600 | tf_op jit(solution)/shard_map/ppermute | solution.py:44
  154.3 19.8 %collective-permute-start.37 = (bf16[1,3216,128]{2,1,0:T(8,128)(2,1)S(1)}, bf16[1,3216,128]{2,1,0:T(8,128)(2,1)S(1)}, u32[]{:S(2)}, u32[]{:S(2)}) collective-permute-start(bf16[1,3216,128]{2,1,0:T(8,128)(2,1)S(1)} %get-tuple-element.164), channel_id=1, source_target_pairs={{0,96},{1,97},{2,98},{3,99},{4,100},{5,101},{6,102},{7,103},{8,104... | collective-permute-start | bytes 2469896 | tf_op jit(solution)/shard_map/ppermute | solution.py:44
  (21 other events, 120.8 us)
where the time goes:
time: 176 us; the launch traced here: 175 us
  waiting for transfers between devices  59.8 us (34%)
  Pallas kernels  55.2 us (31%)
  starting transfers between devices  52.9 us (30%)
  other arithmetic  2.87 us (2%)
  local copies, waits for them, and re-layouts  2.38 us (1%)
  between operations  2.22 us (1%)
    ppermute x42, waiting for transfers between devices, exchange(): return lax.ppermute(value, ('row', 'col'), pairs)  59.8 us
    pallas_call x22, Pallas kernels, call(): pl.pallas_call(kernel, in_specs=specs, out_specs=[vmem()] * len(outs), ou...  55.2 us
    ppermute x42, starting transfers between devices, exchange(): return lax.ppermute(value, ('row', 'col'), pairs)  52.9 us
  transfers between devices with their start and end apart: 42, of which 25 were waited for; matrix products, arithmetic and copies ran while one was open for 2% of the time, Pallas kernels for 25%

commit v1 on v0

--- a/solution.py
+++ b/solution.py
@@ -45,7 +45,6 @@
 
 
 PIECE_OF = [(i // 8, i % 8) for i in range(16)]
-ROW_PIECES = (4, 4)
 NN = ((1,), (0,))
 NT = ((1,), (1,))
 TN = ((0,), (0,))
@@ -57,9 +56,9 @@
 
 def weight_blocks(refs):
     first = 0
-    for n, ref in zip(ROW_PIECES, refs):
-        yield first, n, ref
-        first += n
+    for ref in refs:
+        yield first, ref.shape[0], ref
+        first += ref.shape[0]
 
 
 def weight_of(refs, j):
@@ -143,9 +142,9 @@
 
 def norm_kernel(*refs):
     place = Place()
-    halves, tiny, wts = (refs[0:2], refs[2:4]), refs[4:6], refs[6:8]
-    cos_ref, sa_ref, sb_ref = refs[8:11]
-    normed_ref, qkv_ref, pre_ref, act_ref, cen_ref, inv_ref, gb_ref = refs[11:]
+    halves, tiny, wts = (refs[0:2], refs[2:4]), refs[4:6], refs[6:10]
+    cos_ref, sa_ref, sb_ref = refs[10:13]
+    normed_ref, qkv_ref, pre_ref, act_ref, cen_ref, inv_ref, gb_ref = refs[13:]
 
     lanes = [[place.lane(half, i) for i in range(16)] for half in range(2)]
 
@@ -153,7 +152,7 @@
         return lanes[half][i]
 
     def tiny_of(i):
-        return PIECE_OF[(0, 2, 1, 3)[i // 4] * 4 + i % 4]
+        return PIECE_OF[(0, 8, 2, 10)[i // 4] + (0, 4, 1, 5)[i % 4]]
 
     def tiny_row(i, row):
         a, k = tiny_of(i)
@@ -218,7 +217,7 @@
         shape((8, D), F32),
     ]
     args = (*xa, *xb, *tiny, *wts, cos, sa, sb)
-    return call("norm_proj", norm_kernel, [vmem()] * 11, outs, args)
+    return call("norm_proj", norm_kernel, [vmem()] * 13, outs, args)
 
 
 def head_masks():
@@ -246,8 +245,9 @@
         body(long_start, qi)
 
 
-def attend_kernel(tab, qkv_ref, out_ref):
+def attend_kernel(tab, qkv_ref, out_ref, exact_ref, lse_ref):
     masks = head_masks()
+    low_lanes = lax.broadcasted_iota(jnp.int32, (BLK, 128), 1) < HEAD_DIM
 
     def body(start, qi):
         rows = pl.ds(pl.multiple_of(start + qi * BLK, BLK), BLK)
@@ -256,48 +256,67 @@
         k = qkv_ref[keys, 128:256]
         v = qkv_ref[keys, 256:384]
         total = None
+        logs = []
         for m in masks:
             s = masked_scores(q * m, k, qi)
-            e = jnp.exp(s - jnp.max(s, axis=1, keepdims=True))
-            p = (e * (1.0 / jnp.sum(e, axis=1, keepdims=True))).astype(BF16)
+            most = jnp.max(s, axis=1, keepdims=True)
+            e = jnp.exp(s - most)
+            count = jnp.sum(e, axis=1, keepdims=True)
+            p = (e * (1.0 / count)).astype(BF16)
             o = dot(p, v * m, NN)
             total = o if total is None else total + o
+            logs.append(most + jnp.log(count))
         out_ref[rows, :] = total.astype(BF16)
+        exact_ref[rows, :] = total
+        lse_ref[rows, :] = jnp.where(low_lanes, logs[0], logs[1])
 
     for_blocks(tab, body)
 
 
 def attend_call(tab, qkv):
-    outs = [shape((TOK, 128), BF16)]
-    return call("attend", attend_kernel, [smem(), vmem()], outs, (tab, qkv))[0]
-
-
-def attend_back_kernel(tab, qkv_ref, do_ref, cos_ref, sa_ref, sb_ref, out_ref, sum_ref, dq, dk, dv):
+    outs = [shape((TOK, 128), BF16), shape((TOK, 128), F32), shape((TOK, 128), F32)]
+    return call("attend", attend_kernel, [smem(), vmem()], outs, (tab, qkv))
+
+
+def attend_back_kernel(
+    tab, qkv_ref, do_ref, exact_ref, lse_ref, cos_ref, sa_ref, sb_ref, out_ref, sum_ref, dq, dk, dv
+):
     masks = head_masks()
     dk[...] = jnp.zeros_like(dk)
     dv[...] = jnp.zeros_like(dv)
+    eighth = jnp.asarray(0.125, BF16)
+    causal = lax.broadcasted_iota(jnp.int32, (BLK, BLK), 0) >= lax.broadcasted_iota(jnp.int32, (BLK, BLK), 1)
 
     def body(start, qi):
         rows = pl.ds(pl.multiple_of(start + qi * BLK, BLK), BLK)
-        keys = pl.ds(pl.multiple_of(start, BLK), (qi + 1) * BLK)
         q = qkv_ref[rows, 0:128]
-        k = qkv_ref[keys, 128:256]
-        v = qkv_ref[keys, 256:384]
         do = do_ref[rows, :]
+        weighted = do.astype(F32) * exact_ref[rows, :] * 0.125
+        lse = lse_ref[rows, :]
+        deltas = [jnp.sum(weighted * m.astype(F32), axis=1, keepdims=True) for m in masks]
+        logs = [lse[:, 0:1], lse[:, HEAD_DIM : HEAD_DIM + 1]]
+        qs = [q * m for m in masks]
+        dos = [do * m for m in masks]
+        q_both = jnp.concatenate(qs, axis=0)
+        do_both = jnp.concatenate(dos, axis=0)
         total = None
-        for m in masks:
-            qh = q * m
-            doh = do * m
-            s = masked_scores(qh * jnp.asarray(0.125, BF16), k, qi)
-            e = jnp.exp(s - jnp.max(s, axis=1, keepdims=True))
-            p = e * (1.0 / jnp.sum(e, axis=1, keepdims=True))
-            dp = dot(doh, v, NT)
-            delta = jnp.sum(p * dp, axis=1, keepdims=True)
-            ds = (p * (dp - delta) * 0.125).astype(BF16)
-            part = dot(ds, k * m, NN)
+        for kj in range(qi + 1):
+            keys = pl.ds(pl.multiple_of(start + kj * BLK, BLK), BLK)
+            k = qkv_ref[keys, 128:256]
+            v = qkv_ref[keys, 256:384]
+            ps, dss = [], []
+            for h in range(2):
+                s = dot(qs[h] * eighth, k, NT)
+                if kj == qi:
+                    s = jnp.where(causal, s, -1e30)
+                p = jnp.exp(s - logs[h])
+                dp = dot(dos[h] * eighth, v, NT)
+                dss.append((p * (dp - deltas[h])).astype(BF16))
+                ps.append(p.astype(BF16))
+            part = dot(jnp.concatenate(dss, axis=1), jnp.concatenate([k * m for m in masks], axis=0), NN)
             total = part if total is None else total + part
-            dk[keys, :] += dot(ds, qh, TN)
-            dv[keys, :] += dot(p.astype(BF16), doh, TN)
+            dk[keys, :] += dot(jnp.concatenate(dss, axis=0), q_both, TN)
+            dv[keys, :] += dot(jnp.concatenate(ps, axis=0), do_both, TN)
         dq[rows, :] = total
 
     for_blocks(tab, body)
@@ -310,15 +329,14 @@
         sum_ref[:, s * 128 : (s + 1) * 128] = jnp.broadcast_to(jnp.sum(low.astype(F32), axis=0, keepdims=True), (8, 128))
 
 
-def attend_back_call(tab, qkv, do, cos, sa, sb):
+def attend_back_call(*args):
     outs = [shape((TOK, QKV), BF16), shape((8, QKV), F32)]
     scratch = [pltpu.VMEM((TOK, 128), F32)] * 3
-    args = (tab, qkv, do, cos, sa, sb)
-    return call("attend_back", attend_back_kernel, [smem()] + [vmem()] * 5, outs, args, scratch)
+    return call("attend_back", attend_back_kernel, [smem()] + [vmem()] * 7, outs, args, scratch)
 
 
 def project_kernel(att_ref, act_ref, *refs):
-    wts, outs, whole = refs[0:2], refs[2:6], refs[6]
+    wts, outs, whole = refs[0:4], refs[4:8], refs[8]
     place = Place()
     for half in range(2):
         spots = [[place.spot(half, j, i) for i in range(2)] for j in range(8)]
@@ -340,13 +358,13 @@
 def project_call(att, act, wts):
     outs = [shape((8, HALF, 128), BF16)] * 4
     scratch = [pltpu.VMEM((16, HALF, 128), BF16)]
-    return call("project", project_kernel, [vmem()] * 4, outs, (att, act, *wts), scratch)
+    return call("project", project_kernel, [vmem()] * 6, outs, (att, act, *wts), scratch)
 
 
 def upstream_kernel(*refs):
     place = Place()
-    halves, wts, pre_ref = (refs[0:2], refs[2:4]), refs[4:6], refs[6]
-    g_ref, hid_ref, att_ref, hsum_ref, gsum_ref = refs[7:12]
+    halves, wts, pre_ref = (refs[0:2], refs[2:4]), refs[4:8], refs[8]
+    g_ref, hid_ref, att_ref, hsum_ref, gsum_ref = refs[9:14]
     mine = jnp.zeros((1, 128), F32)
     for half in range(2):
         for i, (a, k) in enumerate(PIECE_OF):
@@ -381,11 +399,11 @@
         shape((8, 128), F32),
     ]
     args = (*ga, *gb, *wts, pre)
-    return call("upstream", upstream_kernel, [vmem()] * 7, outs, args, after=after)
+    return call("upstream", upstream_kernel, [vmem()] * 9, outs, args, after=after)
 
 
 def downstream_kernel(dm_ref, dh_ref, normed_ref, gb_ref, *refs):
-    wts, outs, whole, flat = refs[0:2], refs[2:6], refs[6], refs[7]
+    wts, outs, whole, flat = refs[0:4], refs[4:8], refs[8], refs[9]
     place = Place()
     flat[...] = jnp.zeros_like(flat)
     for half in range(2):
@@ -426,7 +444,7 @@
     outs = [shape((8, HALF + PAD, 128), BF16)] * 4
     scratch = [pltpu.VMEM((16, HALF, 128), BF16), pltpu.VMEM((PAD, 128), F32)]
     args = (dm, dh, normed, gb, *wts)
-    return call("downstream", downstream_kernel, [vmem()] * 6, outs, args, scratch, after)
+    return call("downstream", downstream_kernel, [vmem()] * 8, outs, args, scratch, after)
 
 
 def grad_lanes(p):
@@ -437,17 +455,30 @@
 
 TILE = BLK + PAD
 TILE_TWO = ACT + PAD
-GRAD_ROWS = 7 * TILE + 2 * TILE_TWO
-
-
-def grads_kernel(normed_ref, dm_ref, dh_ref, msum_ref, hsum_ref, att_ref, act_ref, g_ref, gsum_ref, keep, send, turned):
+SPARE = 48
+GRAD_ROWS = 7 * TILE + 2 * TILE_TWO + SPARE
+
+
+def grads_kernel(normed_ref, dm_ref, dh_ref, msum_ref, hsum_ref, att_ref, act_ref, g_ref, gsum_ref, *refs):
+    keep, sends, turned = refs[0], refs[1:5], refs[5]
     turned[0:128, :] = jnp.transpose(att_ref[...])
     turned[128:ACT, :] = jnp.transpose(act_ref[...])
     zero = jnp.zeros((8, 128), F32)
-    for first, out_ref in ((4, send), (0, keep)):
+    for first in (4, 0):
+        if first == 4:
+            def put(p, row, value):
+                n = value.shape[0]
+                while n:
+                    part, at = divmod(row, GRAD_ROWS // 4)
+                    here = min(n, GRAD_ROWS // 4 - at)
+                    sends[part][p, at : at + here, :] = value[:here]
+                    value, row, n = value[here:], row + here, n - here
+        else:
+            def put(p, row, value):
+                keep[p, row : row + value.shape[0], :] = value
 
         @pl.loop(0, 4)
-        def _(p, first=first, out_ref=out_ref):
+        def _(p, first=first, put=put):
             lanes = grad_lanes(first + p)
             block = normed_ref[:, lanes]
             t = 0
@@ -455,21 +486,22 @@
                 part = dot(block, ref[...], TN).astype(BF16)
                 for i in range(n):
                     cut = slice(i * 128, (i + 1) * 128)
-                    out_ref[p, t * TILE : t * TILE + BLK, :] = part[:, cut]
+                    put(p, t * TILE, part[:, cut])
                     sums = jnp.concatenate([sums_ref[:, cut], zero], axis=0).astype(BF16)
-                    out_ref[p, t * TILE + BLK : (t + 1) * TILE, :] = sums
+                    put(p, t * TILE + BLK, sums)
                     t += 1
             part = dot(turned[...], g_ref[:, lanes], NN).astype(BF16)
             sums = jnp.concatenate([gsum_ref[...], zero], axis=0).astype(BF16)
             for i in range(2):
                 at = 7 * TILE + i * TILE_TWO
-                out_ref[p, at : at + ACT, :] = part[:, i * 128 : (i + 1) * 128]
-                out_ref[p, at + ACT : at + TILE_TWO, :] = sums
+                put(p, at, part[:, i * 128 : (i + 1) * 128])
+                put(p, at + ACT, sums)
+            put(p, GRAD_ROWS - SPARE, jnp.zeros((SPARE, 128), BF16))
 
 
 def grads_call(*args, after):
     scratch = [pltpu.VMEM((ACT, TOK), BF16)]
-    return call("grads", grads_kernel, [vmem()] * 9, [shape((4, GRAD_ROWS, 128), BF16)] * 2, args, scratch, after)
+    return call("grads", grads_kernel, [vmem()] * 9, [shape((4, GRAD_ROWS, 128), BF16)] + [shape((4, GRAD_ROWS // 4, 128), BF16)] * 4, args, scratch, after)
 
 
 def fold_part(blocks, out_ref, back_ref, got, keep_out, keep_back, send):
@@ -509,11 +541,9 @@
     return got[0:3], got[3:6], got[6:]
 
 
-def finish_kernel(oa, ba, ga, ob, bb, gb, x_ref, g_ref, cen_ref, inv_ref, small_ref, out_ref, grad_ref, sum_ref):
+def finish_kernel(oa, ba, ga, ob, bb, gb, x_ref, g_ref, cen_ref, inv_ref, small_ref, out_ref, grad_ref):
     gain = small_ref[0:1, :].astype(F32)
     shift = small_ref[2:3, :].astype(F32) + small_ref[3:4, :].astype(F32)
-    total_gain = jnp.zeros((1, 128), F32)
-    total_shift = jnp.zeros((1, 128), F32)
     for half, (o_ref, b_ref, got) in enumerate(((oa, ba, ga), (ob, bb, gb))):
         sums = b_ref[0, HALF : HALF + PAD, :] + got[2 * HALF : 2 * HALF + PAD, :].astype(F32)
         sums = jnp.transpose(sums) * (1.0 / D)
@@ -525,40 +555,50 @@
             out_ref[rows, :] = (x_ref[rows, :].astype(F32) + branch + shift).astype(BF16)
             d = b_ref[0, here, :] + got[there, :].astype(F32)
             cen = cen_ref[rows, :]
-            total_gain = total_gain + jnp.sum(d * cen, axis=0, keepdims=True)
-            total_shift = total_shift + jnp.sum(d, axis=0, keepdims=True)
             m1 = sums[:, 2 * i : 2 * i + 1]
             m2 = sums[:, 2 * i + 1 : 2 * i + 2]
             grad_ref[rows, :] = g_ref[rows, :].astype(F32) + inv_ref[rows, :] * (d * gain - m1 - cen * m2)
-    sum_ref[...] = jnp.concatenate([total_gain, total_shift, jnp.zeros((6, 128), F32)], axis=0)
 
 
 def finish_call(*args):
-    outs = [shape((TOK, 128), BF16), shape((TOK, 128), F32), shape((8, 128), F32)]
+    outs = [shape((TOK, 128), BF16), shape((TOK, 128), F32)]
     return call("finish", finish_kernel, [vmem()] * 11, outs, args, final=True)
 
 
-def fold_row_call(kept, *got, parts=1, after=()):
-    n = got[0].shape[0] // 2
-    cut = GRAD_ROWS // parts
+def norm_sums_kernel(ba, ga, bb, gb, cen_ref, sum_ref):
+    gain = jnp.zeros((1, 128), F32)
+    shift = jnp.zeros((1, 128), F32)
+    for half, (b_ref, got) in enumerate(((ba, ga), (bb, gb))):
+        d = b_ref[0, 0:HALF, :] + got[HALF : 2 * HALF, :].astype(F32)
+        gain = gain + jnp.sum(d * cen_ref[half * HALF : (half + 1) * HALF, :], axis=0, keepdims=True)
+        shift = shift + jnp.sum(d, axis=0, keepdims=True)
+    sum_ref[...] = jnp.concatenate([gain, shift, jnp.zeros((6, 128), F32)], axis=0)
+
+
+def norm_sums_call(*args, after):
+    return call("norm_sums", norm_sums_kernel, [vmem()] * 5, [shape((8, 128), F32)], args, after=after)[0]
+
+
+def fold_core_call(kept, *got):
+    n = GRAD_ROWS // len(got)
 
     def kernel(kept_ref, *refs):
-        ins, keep_ref, sends = refs[: len(got)], refs[len(got)], refs[len(got) + 1 :]
-        step = GRAD_ROWS // len(got)
-        for i in range(n):
-            for m, ref in enumerate(ins):
-                rows = slice(m * step, (m + 1) * step)
+        ins, keep_ref, sends = refs[0 : len(got)], refs[len(got)], refs[len(got) + 1 :]
+        for m, ref in enumerate(ins):
+            rows = slice(m * n, (m + 1) * n)
+            for i in range(2):
                 keep_ref[i, rows, :] = kept_ref[i, rows, :].astype(F32) + ref[i].astype(F32)
-            for m, send in enumerate(sends):
-                rows = slice(m * cut, (m + 1) * cut)
-                if len(got) == 1:
-                    new = ins[0][n + i, rows, :].astype(F32)
-                else:
-                    new = jnp.concatenate([ref[n + i].astype(F32) for ref in ins], axis=0)
-                send[i] = (kept_ref[n + i, rows, :].astype(F32) + new).astype(BF16)
-
-    outs = [shape((n, GRAD_ROWS, 128), F32)] + [shape((n, cut, 128), BF16)] * parts
-    return call("fold_row", kernel, [vmem()] * (1 + len(got)), outs, (kept, *got), after=after)
+                sends[1 - i][0, rows, :] = (kept_ref[2 + i, rows, :].astype(F32) + ref[2 + i].astype(F32)).astype(BF16)
+
+    outs = [shape((2, GRAD_ROWS, 128), F32)] + [shape((1, GRAD_ROWS, 128), BF16)] * 2
+    return call("fold_core", kernel, [vmem()] * (1 + len(got)), outs, (kept, *got))
+
+
+def fold_row_call(kept, got, after):
+    def kernel(kept_ref, got_ref, send_ref):
+        send_ref[0] = (kept_ref[1] + got_ref[0].astype(F32)).astype(BF16)
+
+    return call("fold_row", kernel, [vmem()] * 2, [shape((1, GRAD_ROWS, 128), BF16)], (kept, got), after=after)[0]
 
 
 def lanes_of(v, row, width):
@@ -566,8 +606,11 @@
     return pltpu.roll(v, lax.rem(total - row * width, total), 1)[:, 0:width]
 
 
-def close_kernel(kept_ref, got_ref, qkv_ref, qb_ref, up_ref, ub_ref, out_ref, down_ref, bias_ref, again_ref):
-    total = lambda first, n: kept_ref[0, first : first + n, :] + got_ref[0, first : first + n, :].astype(F32)
+def close_kernel(kept_ref, near_ref, far_ref, qkv_ref, qb_ref, up_ref, ub_ref, out_ref, down_ref, bias_ref, again_ref):
+    def total(first, n):
+        rows = slice(first, first + n)
+        return kept_ref[0, rows, :] + near_ref[0, rows, :].astype(F32) + far_ref[0, rows, :].astype(F32)
+
     row = lax.axis_index("row")
     for s in range(3):
         qkv_ref[s] = total(s * TILE, BLK)
@@ -585,7 +628,7 @@
     again_ref[...] = bias
 
 
-def close_call(kept, got):
+def close_call(*args):
     outs = [
         shape((3, BLK, 128), F32),
         shape((3, 16), F32),
@@ -596,7 +639,7 @@
         shape((1, 16), F32),
         shape((1, 16), F32),
     ]
-    return call("close", close_kernel, [vmem()] * 2, outs, (kept, got), final=True)
+    return call("close", close_kernel, [vmem()] * 3, outs, args, final=True)
 
 
 def close_norm_kernel(*refs):
@@ -608,8 +651,8 @@
     refs[5][...] = mine[1:2]
 
 
-def close_norm_call(*args):
-    return call("close_norm", close_norm_kernel, [vmem()] * 4, [shape((1, 16), F32)] * 2, args, final=True)
+def close_norm_call(*args, after):
+    return call("close_norm", close_norm_kernel, [vmem()] * 4, [shape((1, 16), F32)] * 2, args, after=after, final=True)
 
 
 def join(*groups, after=()):
@@ -658,23 +701,34 @@
     return call("begin", begin_kernel, specs, [shape((2, HALF, 128), BF16)] * 2, in_hbm(*args), scratch, after)
 
 
-def pack_kernel(qkv_ref, up_ref, out_ref, down_ref, cats, twos, out_here, down_here, sem):
+def pack_kernel(qkv_ref, up_ref, out_ref, down_ref, packed, out_here, down_here, sem):
     copies = [
-        pltpu.make_async_copy(qkv_ref.at[s], cats.at[0, :, pl.ds(s * 128, 128)], sem.at[s]) for s in range(3)
+        pltpu.make_async_copy(qkv_ref.at[s], packed.at[0, :, pl.ds(s * 128, 128)], sem.at[s]) for s in range(3)
     ]
-    copies.append(pltpu.make_async_copy(up_ref, cats.at[0, :, pl.ds(QKV, FFL)], sem.at[3]))
+    copies.append(pltpu.make_async_copy(up_ref, packed.at[0, :, pl.ds(QKV, FFL)], sem.at[3]))
     copies.append(pltpu.make_async_copy(out_ref, out_here, sem.at[4]))
     copies.append(pltpu.make_async_copy(down_ref, down_here, sem.at[5]))
     fetch(copies)
-    twos[0, :, 0:128] = jnp.transpose(out_here[...])
-    twos[0, :, 128:ACT] = jnp.transpose(down_here[...])
+    packed[0, :, CAT : CAT + 128] = jnp.transpose(out_here[...])
+    packed[0, :, CAT + 128 : ALL] = jnp.transpose(down_here[...])
 
 
 def pack_call(*args, after):
-    outs = [shape((1, BLK, CAT), BF16), shape((1, BLK, ACT), BF16)]
+    outs = [shape((1, BLK, ALL), BF16)]
     scratch = [pltpu.VMEM((128, BLK), BF16), pltpu.VMEM((FFL, BLK), BF16), pltpu.SemaphoreType.DMA((6,))]
     specs = [pl.BlockSpec(memory_space=pltpu.HBM)] * 4
-    return call("pack", pack_kernel, specs, outs, in_hbm(*args), scratch, after)
+    return call("pack", pack_kernel, specs, outs, in_hbm(*args), scratch, after)[0]
+
+
+def unpack_kernel(mine, got, cats, twos):
+    for i, ref in enumerate((mine, got)):
+        cats[i] = ref[0, :, 0:CAT]
+        twos[i] = ref[0, :, CAT:ALL]
+
+
+def unpack_call(*args):
+    outs = [shape((2, BLK, CAT), BF16), shape((2, BLK, ACT), BF16)]
+    return call("unpack", unpack_kernel, [vmem()] * 2, outs, args)
 
 
 def both(mine, got):
@@ -709,65 +763,67 @@
 
     small = [spread(jnp.stack([gain, shift, b_out, b_down]), 16), spread(b_qkv, 16), spread(b_up, 64)]
     small = jnp.concatenate(small + [jnp.zeros((PAD - 11, 128), BF16)])
+    small = small + exchange(small, "c")
+    weights = pack_call(w_qkv.transpose(1, 0, 2), w_up, w_out, w_down, after=(small,))
+    weights_got = exchange(weights, "z", 0)
     a, b = begin_call(x, g, after=(small,))
     a_got, b_got = exchange(a, "x", 0), exchange(b, "y", 0)
-    small = small + exchange(small, "c")
-    cats, twos = pack_call(w_qkv.transpose(1, 0, 2), w_up, w_out, w_down, after=(small,))
+    small = small + exchange(small, "z", 1)
+    small, a, b = join([small], both(a, a_got), both(b, b_got), after=(weights_got,))
+    a_got, b_got = exchange(a, "x", 1), exchange(b, "y", 1)
+    cats, twos = unpack_call(weights, weights_got)
+    cats_got = exchange(cats, "z", 1)
+    cats = (cats, cats_got, exchange(cats, "c"), exchange(cats_got, "c"))
     small = small + exchange(small, "z", 0)
-    small, cats, twos, a, b = join([small], [cats], [twos], both(a, a_got), both(b, b_got))
-    a_got, b_got = exchange(a, "x", 1), exchange(b, "y", 1)
-    cats_got, twos_got = exchange(cats, "z", 0), exchange(twos, "z", 0)
-    small = small + exchange(small, "z", 1)
-    tiny = small[None]
-    tiny_got = exchange(tiny, "x", 0)
-    tiny, cats, a, b = join([tiny, tiny_got], [cats, cats_got], both(a, a_got), both(b, b_got), after=(twos_got,))
+    tiny, twos, a, b = join([small[None]], [twos], both(a, a_got), both(b, b_got))
     tiny_got = exchange(tiny, "x", 1)
     a_got, b_got = exchange(a, "y", 0), exchange(b, "x", 0)
-    cats_got = exchange(cats, "z", 1)
-    (tiny,) = join([tiny, tiny_got])
+    twos_got = exchange(twos, "z", 1)
+    twos = (twos, twos_got, exchange(twos, "c"), exchange(twos_got, "c"))
+    (tiny,) = join([tiny, tiny_got], after=(cats_got,))
     tiny_got = exchange(tiny, "y", 1)
     first = lambda v, got: [(v, 0, 4), (got, 0, 4)]
     last = lambda v, got: [(v, 4, 8), (got, 4, 8)]
-    tiny, xa, xb, cats, twos, ga, gb = join(
+    tiny, xa, xb, ga, gb = join(
         [tiny, tiny_got],
         first(a, a_got),
         first(b, b_got),
-        [cats, cats_got],
-        [twos, twos_got],
         last(a, a_got),
         last(b, b_got),
+        after=(twos_got, cos, sa, sb),
     )
+    tiny_got = exchange(tiny, "x", 0)
+    xa, xb = (xa, exchange(xa, "y", 1)), (xb, exchange(xb, "x", 1))
+    (tiny,) = join([tiny, tiny_got])
     tiny = (tiny, exchange(tiny, "y", 0))
-    xa, xb = (xa, exchange(xa, "y", 1)), (xb, exchange(xb, "x", 1))
-    cats = (cats, exchange(cats, "c"))
-    twos_got = exchange(twos, "z", 1)
     ga, gb = (ga, exchange(ga, "y", 1)), (gb, exchange(gb, "x", 1))
-    (twos,) = join([twos, twos_got])
-    twos = (twos, exchange(twos, "c"))
 
     normed, qkv, pre, act, centered, inv, gains = norm_call(xa, xb, tiny, cats, cos, sa, sb)
-    att = attend_call(lengths, qkv)
+    att, exact, lse = attend_call(lengths, qkv)
     out_a, send_a, out_b, send_b = project_call(att, act, twos)
     out_a_got, out_b_got = exchange(send_a, "y", 0), exchange(send_b, "x", 0)
     g_all, d_hid, d_att, hsum, gsum = upstream_call(ga, gb, twos, pre, (out_a,))
-    d_mix, msum = attend_back_call(lengths, qkv, d_att, cos, sa, sb)
-    back_a, send_a, back_b, send_b = downstream_call(d_mix, d_hid, normed, gains, cats, (out_a_got, out_b_got))
+    d_mix, msum = attend_back_call(lengths, qkv, d_att, exact, lse, cos, sa, sb)
+    back_a, send_a, back_b, send_b = downstream_call(d_mix, d_hid, normed, gains, cats, ())
     back_a_got, back_b_got = exchange(send_a, "y", 0), exchange(send_b, "x", 0)
-    keep, send = grads_call(normed, d_mix, d_hid, msum, hsum, att, act, g_all, gsum, after=(back_a,))
-    a, b, (send,) = fold_call(8, (out_a, back_a, out_a_got, back_a_got), (out_b, back_b, out_b_got, back_b_got), send)
+    keep, *sends = grads_call(normed, d_mix, d_hid, msum, hsum, att, act, g_all, gsum, after=(back_a, out_a_got, out_b_got))
+    got = [exchange(send, "c") for send in sends]
+    a, b, _ = fold_call(8, (out_a, back_a, out_a_got, back_a_got), (out_b, back_b, out_b_got, back_b_got))
     a_got, b_got = exchange(a[2], "y", 1), exchange(b[2], "x", 1)
-    keep, *sends = fold_row_call(keep, exchange(send, "c"), parts=3)
-    got = [exchange(send, "z", 0) for send in sends]
-    a, b, _ = fold_call(4, (a[0], a[1], a_got), (b[0], b[1], b_got), after=(got[0],))
+    keep, *sends = fold_core_call(keep, *got)
+    first, last = [exchange(send, "z", 0) for send in sends]
+    a, b, _ = fold_call(4, (a[0], a[1], a_got), (b[0], b[1], b_got))
     a_got, b_got = exchange(a[2], "x", 0), exchange(b[2], "y", 0)
-    a, b, _ = fold_call(2, (a[0], a[1], a_got), (b[0], b[1], b_got), after=(got[1],))
+    a, b, _ = fold_call(2, (a[0], a[1], a_got), (b[0], b[1], b_got))
     a_got, b_got = exchange(a[2], "x", 1), exchange(b[2], "y", 1)
-    keep, send = fold_row_call(keep, *got, after=(a[0],))
-    got = exchange(send, "z", 1)
-    block_out, input_grad, sums = finish_call(a[0], a[1], a_got, b[0], b[1], b_got, x, g, centered, inv, small)
+    got = exchange(fold_row_call(keep, first, (a[0],)), "z", 1)
+    sums = norm_sums_call(a[1], a_got, b[1], b_got, centered, after=(last,))
     sums = sums + exchange(sums, "c")
-    gain_grad, shift_grad = close_norm_call(sums, *(exchange(sums, "z", n) for n in range(3)))
-    qkv_grad, qkv_bias, up_grad, up_bias, out_grad, down_grad, out_bias, down_bias = close_call(keep, got)
+    block_out, input_grad = finish_call(a[0], a[1], a_got, b[0], b[1], b_got, x, g, centered, inv, small)
+    qkv_grad, qkv_bias, up_grad, up_bias, out_grad, down_grad, out_bias, down_bias = close_call(keep, last, got)
+    gain_grad, shift_grad = close_norm_call(
+        sums, *(exchange(sums, "z", n) for n in range(3)), after=in_hbm(up_grad, input_grad)
+    )
     return (
         block_out,
         input_grad,

time: 176 us -> 171 us (0.972)
  waiting for transfers between devices: 59.8 us -> 39 us
  starting transfers between devices: 52.9 us -> 71.4 us
  Pallas kernels: 55.2 us -> 52.8 us
    ppermute x42 -> x45, waiting for transfers between devices: 59.8 us -> 39 us  [exchange(): return lax.ppermute(value, ('row', 'col'), pairs)]
    ppermute x42 -> x45, starting transfers between devices: 52.9 us -> 71.4 us  [exchange(): return lax.ppermute(value, ('row', 'col'), pairs)]
    pallas_call x22 -> x24, Pallas kernels: 55.2 us -> 52.8 us  [call(): pl.pallas_call(kernel, in_specs=specs, out_specs=[vmem()] * len(outs), ou...]
  transfers between devices with their start and end apart: 42 -> 45, of which waited for: 25 -> 18; matrix products, arithmetic and copies ran while one was open for 2% -> 2% of each run, Pallas kernels for 25% -> 30%
where the time goes in v1:
time: 171 us
  starting transfers between devices  71.4 us (42%)
  Pallas kernels  52.8 us (31%)
  waiting for transfers between devices  39 us (23%)
  other arithmetic  2.86 us (2%)
  local copies, waits for them, and re-layouts  2.38 us (1%)
  between operations  2.24 us (1%)
    ppermute x45, starting transfers between devices, exchange(): return lax.ppermute(value, ('row', 'col'), pairs)  71.4 us
    pallas_call x24, Pallas kernels, call(): pl.pallas_call(kernel, in_specs=specs, out_specs=[vmem()] * len(outs), ou...  52.8 us
    ppermute x45, waiting for transfers between devices, exchange(): return lax.ppermute(value, ('row', 'col'), pairs)  39 us
  transfers between devices with their start and end apart: 45, of which 18 were waited for; matrix products, arithmetic and copies ran while one was open for 2% of the time, Pallas kernels for 30%

profile of v1, /device:TPU:1, one launch (start us, length us, event | category | flops | bytes accessed | tf_op | source)
XLA Modules:
  0.0 170.7 jit_solution(2931694145112283557)
XLA Ops:
  7.0 3.9 %collective-permute-start.4 = (bf16[1,256,1536]{2,1,0:T(8,128)(2,1)S(1)}, bf16[1,256,1536]{2,1,0:T(8,128)(2,1)S(1)}, u32[]{:S(2)}, u32[]{:S(2)}) collective-permute-start(bf16[1,256,1536]{2,1,0:T(8,128)(2,1)S(1)} %pack.1.mine), channel_id=1, source_target_pairs={{0,32},{1,33},{2,34},{3,35},{4,36},{5,37},{6,38},{7,39},{8,40},{9,... | collective-permute-start | bytes 2359304 | tf_op jit(solution)/shard_map/ppermute | solution.py:44
  12.0 2.6 %collective-permute-start.2 = (bf16[2,512,128]{2,1,0:T(8,128)(2,1)S(1)}, bf16[2,512,128]{2,1,0:T(8,128)(2,1)S(1)}, u32[]{:S(2)}, u32[]{:S(2)}) collective-permute-start(bf16[2,512,128]{2,1,0:T(8,128)(2,1)S(1)} %get-tuple-element.91.refs_1_.refs_3_), channel_id=1, source_target_pairs={{0,1},{1,0},{2,3},{3,2},{4,5},{5,4},{6,7},{7,6},{8,9},{9,8},{10,11... | collective-permute-start | bytes 786440 | tf_op jit(solution)/shard_map/ppermute | solution.py:44
  14.6 2.7 %collective-permute-start.3 = (bf16[2,512,128]{2,1,0:T(8,128)(2,1)S(1)}, bf16[2,512,128]{2,1,0:T(8,128)(2,1)S(1)}, u32[]{:S(2)}, u32[]{:S(2)}) collective-permute-start(bf16[2,512,128]{2,1,0:T(8,128)(2,1)S(1)} %get-tuple-element.92.refs_5_.refs_7_), channel_id=1, source_target_pairs={{0,4},{1,5},{2,6},{3,7},{4,0},{5,1},{6,2},{7,3},{8,12},{9,13},{10,... | collective-permute-start | bytes 786440 | tf_op jit(solution)/shard_map/ppermute | solution.py:44
  17.3 2.5 %collective-permute-done.1 = bf16[16,128]{1,0:T(8,128)(2,1)S(1)} collective-permute-done((bf16[16,128]{1,0:T(8,128)(2,1)S(1)}, bf16[16,128]{1,0:T(8,128)(2,1)S(1)}, u32[]{:S(2)}, u32[]{:S(2)}) %collective-permute-start.1) | collective-permute-done | bytes 4128 | tf_op jit(solution)/shard_map/ppermute | solution.py:44
  23.2 2.7 %collective-permute-start.5 = (bf16[16,128]{1,0:T(8,128)(2,1)S(1)}, bf16[16,128]{1,0:T(8,128)(2,1)S(1)}, u32[]{:S(2)}, u32[]{:S(2)}) collective-permute-start(bf16[16,128]{1,0:T(8,128)(2,1)S(1)} %get-tuple-element.93), channel_id=1, source_target_pairs={{0,32},{1,33},{2,34},{3,35},{4,36},{5,37},{6,38},{7,39},{8,40},{9,... | collective-permute-start | bytes 12296 | tf_op jit(solution)/shard_map/ppermute | solution.py:44
  30.2 2.8 %collective-permute-start.11 = (bf16[8,512,128]{2,1,0:T(8,128)(2,1)S(1)}, bf16[8,512,128]{2,1,0:T(8,128)(2,1)S(1)}, u32[]{:S(2)}, u32[]{:S(2)}) collective-permute-start(bf16[8,512,128]{2,1,0:T(8,128)(2,1)S(1)} %get-tuple-element.99.refs_2_.refs_6_), channel_id=1, source_target_pairs={{0,4},{1,5},{2,6},{3,7},{4,0},{5,1},{6,2},{7,3},{8,12},{9,13},{10,... | collective-permute-start | bytes 3145736 | tf_op jit(solution)/shard_map/ppermute | solution.py:44
  37.1 2.5 %collective-permute-done.8.refs_1_ = bf16[1,16,128]{2,1,0:T(8,128)(2,1)S(1)} collective-permute-done((bf16[1,16,128]{2,1,0:T(8,128)(2,1)S(1)}, bf16[1,16,128]{2,1,0:T(8,128)(2,1)S(1)}, u32[]{:S(2)}, u32[]{:S(2)}) %collective-permute-start.8) | collective-permute-done | bytes 4128 | tf_op jit(solution)/shard_map/ppermute | solution.py:44
  39.7 4.9 %collective-permute-start.18 = (bf16[2,256,896]{2,1,0:T(8,128)(2,1)S(1)}, bf16[2,256,896]{2,1,0:T(8,128)(2,1)S(1)}, u32[]{:S(2)}, u32[]{:S(2)}) collective-permute-start(bf16[2,256,896]{2,1,0:T(8,128)(2,1)S(1)} %get-tuple-element.98.refs_6_.refs_0_), channel_id=1, source_target_pairs={{0,16},{1,17},{2,18},{3,19},{4,20},{5,21},{6,22},{7,23},{8,24},{9,... | collective-permute-start | bytes 2752520 | tf_op jit(solution)/shard_map/ppermute | solution.py:44
  49.5 4.3 %collective-permute-start.19 = (bf16[2,256,896]{2,1,0:T(8,128)(2,1)S(1)}, bf16[2,256,896]{2,1,0:T(8,128)(2,1)S(1)}, u32[]{:S(2)}, u32[]{:S(2)}) collective-permute-start(bf16[2,256,896]{2,1,0:T(8,128)(2,1)S(1)} %collective-permute-done.9.refs_2_.refs_7_.refs_1_), channel_id=1, source_target_pairs={{0,16},{1,17},{2,18},{3,19},{4,20},{5,21},{6,22},{7,23},{8,24},{9,... | collective-permute-start | bytes 2752520 | tf_op jit(solution)/shard_map/ppermute | solution.py:44
  58.3 4.5 %collective-permute-done.17.refs_5_ = bf16[8,16,128]{2,1,0:T(8,128)(2,1)S(1)} collective-permute-done((bf16[8,16,128]{2,1,0:T(8,128)(2,1)S(1)}, bf16[8,16,128]{2,1,0:T(8,128)(2,1)S(1)}, u32[]{:S(2)}, u32[]{:S(2)}) %collective-permute-start.17) | collective-permute-done | bytes 32800 | tf_op jit(solution)/shard_map/ppermute | solution.py:44
  63.3 9.3 %norm_proj.1 = (bf16[1024,2048]{1,0:T(8,128)(2,1)S(1)}, bf16[1024,384]{1,0:T(8,128)(2,1)S(1)}, f32[1024,512]{1,0:T(8,128)S(1)}, bf16[1024,512]{1,0:T(8,128)(2,1)...) custom-call(bf16[8,512,128]{2,1,0:T(8,128)(2,1)S(1)} %get-tuple-element.102.refs_0_, ...), custom_call_target="tpu_custom_call" | custom-call | flops 2249999872 | tf_op jit(solution)/shard_map/norm_proj/pallas_call | solution.py:131
  72.6 3.3 %attend.1 = (bf16[1024,128]{1,0:T(8,128)(2,1)S(1)}, f32[1024,128]{1,0:T(8,128)S(1)}, f32[1024,128]{1,0:T(8,128)S(1)}) custom-call(s32[1,2]{1,0:T(1,128)S(1)} %copy-done.2, bf16[1024,384]{1,0:T(8,128)(2,1)S(1)} %get-tuple-element.105.qkv_ref), custom_call_target="tpu_custom_call" | custom-call | flops 750000000 | tf_op jit(solution)/shard_map/attend/pallas_call | solution.py:131
  75.9 4.6 %project.1 = (bf16[8,512,128]{2,1,0:T(8,128)(2,1)S(1)}, bf16[8,512,128]{2,1,0:T(8,128)(2,1)S(1)}, bf16[8,512,128]{2,1,0:T(8,128)(2,1)S(1)}, bf16[8,512,128]{2,1,0:T(8,128)(2,1)S(1)}) custom-call(bf16[1024,128]{1,0:T(8,128)(2,1)S(1)} %get-tuple-element.106.att_ref.refs_5_, bf16[1024,512]{1,0:T(8,128)(2,1)S(1)} %get-tuple-element.107.act_ref.refs_6_, ...), custom_call_target="tpu_custom_call" | custom-call | flops 1250000000 | tf_op jit(solution)/shard_map/project/pallas_call | solution.py:131
  80.5 2.8 %collective-permute-start.24 = (bf16[8,512,128]{2,1,0:T(8,128)(2,1)S(1)}, bf16[8,512,128]{2,1,0:T(8,128)(2,1)S(1)}, u32[]{:S(2)}, u32[]{:S(2)}) collective-permute-start(bf16[8,512,128]{2,1,0:T(8,128)(2,1)S(1)} %get-tuple-element.120), channel_id=1, source_target_pairs={{0,4},{1,5},{2,6},{3,7},{4,0},{5,1},{6,2},{7,3},{8,12},{9,13},{10,... | collective-permute-start | bytes 3145736 | tf_op jit(solution)/shard_map/ppermute | solution.py:44
  84.0 6.1 %upstream.1 = (bf16[1024,2048]{1,0:T(8,128)(2,1)S(1)}, bf16[1024,512]{1,0:T(8,128)(2,1)S(1)}, bf16[1024,128]{1,0:T(8,128)(2,1)S(1)}, f32[8,512]{1,0:T(8,128)S(1)}, f32[8,128]{1,0:T(8,128)S(1)}) custom-call(bf16[8,512,128]{2,1,0:T(8,128)(2,1)S(1)} %get-tuple-element.109.refs_0_, bf16[8,512,128]{2,1,0:T(8,128)(2,1)S(1)} %collective-permute-done.22.refs_1_, ...), custom_call_target="tpu_custom_call" | custom-call | flops 1500000000 | tf_op jit(solution)/shard_map/upstream/pallas_call | solution.py:131
  90.1 5.1 %attend_back.1 = (bf16[1024,384]{1,0:T(8,128)(2,1)S(1)}, f32[8,384]{1,0:T(8,128)S(1)}) custom-call(s32[1,2]{1,0:T(1,128)S(1)} %copy-done.2, bf16[1024,384]{1,0:T(8,128)(2,1)S(1)} %get-tuple-element.105.qkv_ref, bf16[1024,128]{1,0:T(8,128)(2,1)S(1)} %get-tuple-element.112.do_ref, f32[1024,128]{1,0:T(8,128)S(1)} %get-tuple-element.113.exact_ref, ...), custom_call_target="tpu_custom_call" | custom-call | flops 1750000000 | tf_op jit(solution)/shard_map/attend_back/pallas_call | solution.py:131
  95.1 6.5 %downstream.1 = (bf16[8,528,128]{2,1,0:T(8,128)(2,1)S(1)}, bf16[8,528,128]{2,1,0:T(8,128)(2,1)S(1)}, bf16[8,528,128]{2,1,0:T(8,128)(2,1)S(1)}, bf16[8,528,128]{2,1,0:T(8,128)(2,1)S(1)}) custom-call(bf16[1024,384]{1,0:T(8,128)(2,1)S(1)} %get-tuple-element.115.dm_ref.refs_1_, bf16[1024,512]{1,0:T(8,128)(2,1)S(1)} %get-tuple-element.116.dh_ref.refs_2_, ...), custom_call_target="tpu_custom_call" | custom-call | flops 1500000000 | tf_op jit(solution)/shard_map/downstream/pallas_call | solution.py:131
  103.8 9.2 %grads.1 = (bf16[4,3264,128]{2,1,0:T(8,128)(2,1)S(1)}, bf16[4,816,128]{2,1,0:T(8,128)(2,1)S(1)}, bf16[4,816,128]{2,1,0:T(8,128)(2,1)S(1)}, bf16[4,816,128]{2,1,0:T(8,128)(2,1)S(1)}, bf16[4,816,128]{2,1,0:T(8,128)(2,1)S(1)}) custom-call(bf16[1024,2048]{1,0:T(8,128)(2,1)S(1)} %get-tuple-element.117.normed_ref.refs_0_, ...), custom_call_target="tpu_custom_call" | custom-call | flops 2750000128 | tf_op jit(solution)/shard_map/grads/pallas_call | solution.py:131
  113.1 4.3 %collective-permute-start.34 = (bf16[4,816,128]{2,1,0:T(8,128)(2,1)S(1)}, bf16[4,816,128]{2,1,0:T(8,128)(2,1)S(1)}, u32[]{:S(2)}, u32[]{:S(2)}) collective-permute-start(bf16[4,816,128]{2,1,0:T(8,128)(2,1)S(1)} %get-tuple-element.153), channel_id=1, source_target_pairs={{0,16},{1,17},{2,18},{3,19},{4,20},{5,21},{6,22},{7,23},{8,24},{9,... | collective-permute-start | bytes 2506760 | tf_op jit(solution)/shard_map/ppermute | solution.py:44
  126.7 7.8 %collective-permute-done.28.refs_2_ = bf16[4160,128]{1,0:T(8,128)(2,1)S(1)} collective-permute-done((bf16[4160,128]{1,0:T(8,128)(2,1)S(1)}, bf16[4160,128]{1,0:T(8,128)(2,1)S(1)}, u32[]{:S(2)}, u32[]{:S(2)}) %collective-permute-start.28) | collective-permute-done | bytes 1064992 | tf_op jit(solution)/shard_map/ppermute | solution.py:44
  141.9 4.1 %collective-permute-done.30.refs_2_ = bf16[2080,128]{1,0:T(8,128)(2,1)S(1)} collective-permute-done((bf16[2080,128]{1,0:T(8,128)(2,1)S(1)}, bf16[2080,128]{1,0:T(8,128)(2,1)S(1)}, u32[]{:S(2)}, u32[]{:S(2)}) %collective-permute-start.30) | collective-permute-done | bytes 532512 | tf_op jit(solution)/shard_map/ppermute | solution.py:44
  148.3 3.9 %collective-permute-done.38.near_ref.refs_5_ = bf16[1,3264,128]{2,1,0:T(8,128)(2,1)S(1)} collective-permute-done((bf16[1,3264,128]{2,1,0:T(8,128)(2,1)S(1)}, bf16[1,3264,128]{2,1,0:T(8,128)(2,1)S(1)}, u32[]{:S(2)}, u32[]{:S(2)}) %collective-permute-start.38) | collective-permute-done | bytes 835616 | tf_op jit(solution)/shard_map/ppermute | solution.py:44
  154.0 9.4 %collective-permute-start.41 = (f32[8,128]{1,0:T(8,128)S(1)}, f32[8,128]{1,0:T(8,128)S(1)}, u32[]{:S(2)}, u32[]{:S(2)}) collective-permute-start(f32[8,128]{1,0:T(8,128)S(1)} %norm_sums.1), channel_id=1, source_target_pairs={{0,16},{1,17},{2,18},{3,19},{4,20},{5,21},{6,22},{7,23},{8,24},{9,... | collective-permute-start | bytes 12296 | tf_op jit(solution)/shard_map/ppermute | solution.py:44
  165.0 2.5 %collective-permute-start.42 = (f32[8,128]{1,0:T(8,128)S(1)}, f32[8,128]{1,0:T(8,128)S(1)}, u32[]{:S(2)}, u32[]{:S(2)}) collective-permute-start(f32[8,128]{1,0:T(8,128)S(1)} %add.56.refs_0_), channel_id=1, source_target_pairs={{0,32},{1,33},{2,34},{3,35},{4,36},{5,37},{6,38},{7,39},{8,40},{9,... | collective-permute-start | bytes 12296 | tf_op jit(solution)/shard_map/ppermute | solution.py:44
  (121 shorter events, 56.3 us)
Async XLA Ops:
  7.0 14.1 %collective-permute-start.4 = (bf16[1,256,1536]{2,1,0:T(8,128)(2,1)S(1)}, bf16[1,256,1536]{2,1,0:T(8,128)(2,1)S(1)}, u32[]{:S(2)}, u32[]{:S(2)}) collective-permute-start(bf16[1,256,1536]{2,1,0:T(8,128)(2,1)S(1)} %pack.1.mine), channel_id=1, source_target_pairs={{0,32},{1,33},{2,34},{3,35},{4,36},{5,37},{6,38},{7,39},{8,40},{9,... | collective-permute-start | bytes 2359304 | tf_op jit(solution)/shard_map/ppermute | solution.py:44
  23.1 21.5 %collective-permute-start.9 = (bf16[2,256,896]{2,1,0:T(8,128)(2,1)S(1)}, bf16[2,256,896]{2,1,0:T(8,128)(2,1)S(1)}, u32[]{:S(2)}, u32[]{:S(2)}) collective-permute-start(bf16[2,256,896]{2,1,0:T(8,128)(2,1)S(1)} %get-tuple-element.98.refs_6_.refs_0_), channel_id=1, source_target_pairs={{0,96},{1,97},{2,98},{3,99},{4,100},{5,101},{6,102},{7,103},{8,104... | collective-permute-start | bytes 2752520 | tf_op jit(solution)/shard_map/ppermute | solution.py:44
  30.2 17.8 %collective-permute-start.11 = (bf16[8,512,128]{2,1,0:T(8,128)(2,1)S(1)}, bf16[8,512,128]{2,1,0:T(8,128)(2,1)S(1)}, u32[]{:S(2)}, u32[]{:S(2)}) collective-permute-start(bf16[8,512,128]{2,1,0:T(8,128)(2,1)S(1)} %get-tuple-element.99.refs_2_.refs_6_), channel_id=1, source_target_pairs={{0,4},{1,5},{2,6},{3,7},{4,0},{5,1},{6,2},{7,3},{8,12},{9,13},{10,... | collective-permute-start | bytes 3145736 | tf_op jit(solution)/shard_map/ppermute | solution.py:44
  33.0 15.0 %collective-permute-start.12 = (bf16[8,512,128]{2,1,0:T(8,128)(2,1)S(1)}, bf16[8,512,128]{2,1,0:T(8,128)(2,1)S(1)}, u32[]{:S(2)}, u32[]{:S(2)}) collective-permute-start(bf16[8,512,128]{2,1,0:T(8,128)(2,1)S(1)} %get-tuple-element.100.refs_4_.refs_8_), channel_id=1, source_target_pairs={{0,1},{1,0},{2,3},{3,2},{4,5},{5,4},{6,7},{7,6},{8,9},{9,8},{10,11... | collective-permute-start | bytes 3145736 | tf_op jit(solution)/shard_map/ppermute | solution.py:44
  35.4 12.6 %collective-permute-start.13 = (bf16[2,256,640]{2,1,0:T(8,128)(2,1)S(1)}, bf16[2,256,640]{2,1,0:T(8,128)(2,1)S(1)}, u32[]{:S(2)}, u32[]{:S(2)}) collective-permute-start(bf16[2,256,640]{2,1,0:T(8,128)(2,1)S(1)} %get-tuple-element.101.refs_0_.refs_4_), channel_id=1, source_target_pairs={{0,96},{1,97},{2,98},{3,99},{4,100},{5,101},{6,102},{7,103},{8,104... | collective-permute-start | bytes 1966088 | tf_op jit(solution)/shard_map/ppermute | solution.py:44
  39.7 18.6 %collective-permute-start.18 = (bf16[2,256,896]{2,1,0:T(8,128)(2,1)S(1)}, bf16[2,256,896]{2,1,0:T(8,128)(2,1)S(1)}, u32[]{:S(2)}, u32[]{:S(2)}) collective-permute-start(bf16[2,256,896]{2,1,0:T(8,128)(2,1)S(1)} %get-tuple-element.98.refs_6_.refs_0_), channel_id=1, source_target_pairs={{0,16},{1,17},{2,18},{3,19},{4,20},{5,21},{6,22},{7,23},{8,24},{9,... | collective-permute-start | bytes 2752520 | tf_op jit(solution)/shard_map/ppermute | solution.py:44
  48.3 14.5 %collective-permute-start.14 = (bf16[8,512,128]{2,1,0:T(8,128)(2,1)S(1)}, bf16[8,512,128]{2,1,0:T(8,128)(2,1)S(1)}, u32[]{:S(2)}, u32[]{:S(2)}) collective-permute-start(bf16[8,512,128]{2,1,0:T(8,128)(2,1)S(1)} %get-tuple-element.102.refs_0_), channel_id=1, source_target_pairs={{0,12},{1,13},{2,14},{3,15},{4,8},{5,9},{6,10},{7,11},{8,4},{9,5},... | collective-permute-start | bytes 3145736 | tf_op jit(solution)/shard_map/ppermute | solution.py:44
  49.2 14.1 %collective-permute-start.15 = (bf16[8,512,128]{2,1,0:T(8,128)(2,1)S(1)}, bf16[8,512,128]{2,1,0:T(8,128)(2,1)S(1)}, u32[]{:S(2)}, u32[]{:S(2)}) collective-permute-start(bf16[8,512,128]{2,1,0:T(8,128)(2,1)S(1)} %get-tuple-element.103.refs_2_), channel_id=1, source_target_pairs={{0,3},{1,2},{2,1},{3,0},{4,7},{5,6},{6,5},{7,4},{8,11},{9,10},{10,... | collective-permute-start | bytes 3145736 | tf_op jit(solution)/shard_map/ppermute | solution.py:44
  49.5 13.3 %collective-permute-start.19 = (bf16[2,256,896]{2,1,0:T(8,128)(2,1)S(1)}, bf16[2,256,896]{2,1,0:T(8,128)(2,1)S(1)}, u32[]{:S(2)}, u32[]{:S(2)}) collective-permute-start(bf16[2,256,896]{2,1,0:T(8,128)(2,1)S(1)} %collective-permute-done.9.refs_2_.refs_7_.refs_1_), channel_id=1, source_target_pairs={{0,16},{1,17},{2,18},{3,19},{4,20},{5,21},{6,22},{7,23},{8,24},{9,... | collective-permute-start | bytes 2752520 | tf_op jit(solution)/shard_map/ppermute | solution.py:44
  58.3 17.6 %collective-permute-start.20 = (bf16[2,256,640]{2,1,0:T(8,128)(2,1)S(1)}, bf16[2,256,640]{2,1,0:T(8,128)(2,1)S(1)}, u32[]{:S(2)}, u32[]{:S(2)}) collective-permute-start(bf16[2,256,640]{2,1,0:T(8,128)(2,1)S(1)} %get-tuple-element.101.refs_0_.refs_4_), channel_id=1, source_target_pairs={{0,16},{1,17},{2,18},{3,19},{4,20},{5,21},{6,22},{7,23},{8,24},{9,... | collective-permute-start | bytes 1966088 | tf_op jit(solution)/shard_map/ppermute | solution.py:44
  62.7 13.1 %collective-permute-start.21 = (bf16[2,256,640]{2,1,0:T(8,128)(2,1)S(1)}, bf16[2,256,640]{2,1,0:T(8,128)(2,1)S(1)}, u32[]{:S(2)}, u32[]{:S(2)}) collective-permute-start(bf16[2,256,640]{2,1,0:T(8,128)(2,1)S(1)} %collective-permute-done.13.refs_10_.refs_1_.refs_5_), channel_id=1, source_target_pairs={{0,16},{1,17},{2,18},{3,19},{4,20},{5,21},{6,22},{7,23},{8,24},{9,... | collective-permute-start | bytes 1966088 | tf_op jit(solution)/shard_map/ppermute | solution.py:44
  62.8 21.2 %collective-permute-start.22 = (bf16[8,512,128]{2,1,0:T(8,128)(2,1)S(1)}, bf16[8,512,128]{2,1,0:T(8,128)(2,1)S(1)}, u32[]{:S(2)}, u32[]{:S(2)}) collective-permute-start(bf16[8,512,128]{2,1,0:T(8,128)(2,1)S(1)} %get-tuple-element.109.refs_0_), channel_id=1, source_target_pairs={{0,12},{1,13},{2,14},{3,15},{4,8},{5,9},{6,10},{7,11},{8,4},{9,5},... | collective-permute-start | bytes 3145736 | tf_op jit(solution)/shard_map/ppermute | solution.py:44
  62.8 21.2 %collective-permute-start.23 = (bf16[8,512,128]{2,1,0:T(8,128)(2,1)S(1)}, bf16[8,512,128]{2,1,0:T(8,128)(2,1)S(1)}, u32[]{:S(2)}, u32[]{:S(2)}) collective-permute-start(bf16[8,512,128]{2,1,0:T(8,128)(2,1)S(1)} %get-tuple-element.110.refs_2_), channel_id=1, source_target_pairs={{0,3},{1,2},{2,1},{3,0},{4,7},{5,6},{6,5},{7,4},{8,11},{9,10},{10,... | collective-permute-start | bytes 3145736 | tf_op jit(solution)/shard_map/ppermute | solution.py:44
  80.5 23.3 %collective-permute-start.24 = (bf16[8,512,128]{2,1,0:T(8,128)(2,1)S(1)}, bf16[8,512,128]{2,1,0:T(8,128)(2,1)S(1)}, u32[]{:S(2)}, u32[]{:S(2)}) collective-permute-start(bf16[8,512,128]{2,1,0:T(8,128)(2,1)S(1)} %get-tuple-element.120), channel_id=1, source_target_pairs={{0,4},{1,5},{2,6},{3,7},{4,0},{5,1},{6,2},{7,3},{8,12},{9,13},{10,... | collective-permute-start | bytes 3145736 | tf_op jit(solution)/shard_map/ppermute | solution.py:44
  83.3 20.5 %collective-permute-start.26 = (bf16[8,512,128]{2,1,0:T(8,128)(2,1)S(1)}, bf16[8,512,128]{2,1,0:T(8,128)(2,1)S(1)}, u32[]{:S(2)}, u32[]{:S(2)}) collective-permute-start(bf16[8,512,128]{2,1,0:T(8,128)(2,1)S(1)} %get-tuple-element.124), channel_id=1, source_target_pairs={{0,1},{1,0},{2,3},{3,2},{4,5},{5,4},{6,7},{7,6},{8,9},{9,8},{10,11... | collective-permute-start | bytes 3145736 | tf_op jit(solution)/shard_map/ppermute | solution.py:44
  101.6 16.2 %collective-permute-start.25 = (bf16[8,528,128]{2,1,0:T(8,128)(2,1)S(1)}, bf16[8,528,128]{2,1,0:T(8,128)(2,1)S(1)}, u32[]{:S(2)}, u32[]{:S(2)}) collective-permute-start(bf16[8,528,128]{2,1,0:T(8,128)(2,1)S(1)} %get-tuple-element.121), channel_id=1, source_target_pairs={{0,4},{1,5},{2,6},{3,7},{4,0},{5,1},{6,2},{7,3},{8,12},{9,13},{10,... | collective-permute-start | bytes 3244040 | tf_op jit(solution)/shard_map/ppermute | solution.py:44
  102.9 16.4 %collective-permute-start.27 = (bf16[8,528,128]{2,1,0:T(8,128)(2,1)S(1)}, bf16[8,528,128]{2,1,0:T(8,128)(2,1)S(1)}, u32[]{:S(2)}, u32[]{:S(2)}) collective-permute-start(bf16[8,528,128]{2,1,0:T(8,128)(2,1)S(1)} %get-tuple-element.125), channel_id=1, source_target_pairs={{0,1},{1,0},{2,3},{3,2},{4,5},{5,4},{6,7},{7,6},{8,9},{9,8},{10,11... | collective-permute-start | bytes 3244040 | tf_op jit(solution)/shard_map/ppermute | solution.py:44
  120.1 14.4 %collective-permute-start.28 = (bf16[4160,128]{1,0:T(8,128)(2,1)S(1)}, bf16[4160,128]{1,0:T(8,128)(2,1)S(1)}, u32[]{:S(2)}, u32[]{:S(2)}) collective-permute-start(bf16[4160,128]{1,0:T(8,128)(2,1)S(1)} %get-tuple-element.128), channel_id=1, source_target_pairs={{0,12},{1,13},{2,14},{3,15},{4,8},{5,9},{6,10},{7,11},{8,4},{9,5},... | collective-permute-start | bytes 3194888 | tf_op jit(solution)/shard_map/ppermute | solution.py:44
  121.8 14.4 %collective-permute-start.29 = (bf16[4160,128]{1,0:T(8,128)(2,1)S(1)}, bf16[4160,128]{1,0:T(8,128)(2,1)S(1)}, u32[]{:S(2)}, u32[]{:S(2)}) collective-permute-start(bf16[4160,128]{1,0:T(8,128)(2,1)S(1)} %get-tuple-element.131), channel_id=1, source_target_pairs={{0,3},{1,2},{2,1},{3,0},{4,7},{5,6},{6,5},{7,4},{8,11},{9,10},{10,... | collective-permute-start | bytes 3194888 | tf_op jit(solution)/shard_map/ppermute | solution.py:44
  124.3 22.7 %collective-permute-start.39 = (bf16[1,3264,128]{2,1,0:T(8,128)(2,1)S(1)}, bf16[1,3264,128]{2,1,0:T(8,128)(2,1)S(1)}, u32[]{:S(2)}, u32[]{:S(2)}) collective-permute-start(bf16[1,3264,128]{2,1,0:T(8,128)(2,1)S(1)} %get-tuple-element.159), channel_id=1, source_target_pairs={{0,32},{1,33},{2,34},{3,35},{4,36},{5,37},{6,38},{7,39},{8,40},{9,... | collective-permute-start | bytes 2506760 | tf_op jit(solution)/shard_map/ppermute | solution.py:44
  136.6 9.4 %collective-permute-start.30 = (bf16[2080,128]{1,0:T(8,128)(2,1)S(1)}, bf16[2080,128]{1,0:T(8,128)(2,1)S(1)}, u32[]{:S(2)}, u32[]{:S(2)}) collective-permute-start(bf16[2080,128]{1,0:T(8,128)(2,1)S(1)} %get-tuple-element.134), channel_id=1, source_target_pairs={{0,1},{1,0},{2,3},{3,2},{4,5},{5,4},{6,7},{7,6},{8,9},{9,8},{10,11... | collective-permute-start | bytes 1597448 | tf_op jit(solution)/shard_map/ppermute | solution.py:44
  139.6 12.6 %collective-permute-start.38 = (bf16[1,3264,128]{2,1,0:T(8,128)(2,1)S(1)}, bf16[1,3264,128]{2,1,0:T(8,128)(2,1)S(1)}, u32[]{:S(2)}, u32[]{:S(2)}) collective-permute-start(bf16[1,3264,128]{2,1,0:T(8,128)(2,1)S(1)} %get-tuple-element.158), channel_id=1, source_target_pairs={{0,32},{1,33},{2,34},{3,35},{4,36},{5,37},{6,38},{7,39},{8,40},{9,... | collective-permute-start | bytes 2506760 | tf_op jit(solution)/shard_map/ppermute | solution.py:44
  147.1 21.7 %collective-permute-start.40 = (bf16[1,3264,128]{2,1,0:T(8,128)(2,1)S(1)}, bf16[1,3264,128]{2,1,0:T(8,128)(2,1)S(1)}, u32[]{:S(2)}, u32[]{:S(2)}) collective-permute-start(bf16[1,3264,128]{2,1,0:T(8,128)(2,1)S(1)} %fold_row.1), channel_id=1, source_target_pairs={{0,96},{1,97},{2,98},{3,99},{4,100},{5,101},{6,102},{7,103},{8,104... | collective-permute-start | bytes 2506760 | tf_op jit(solution)/shard_map/ppermute | solution.py:44
  154.0 10.2 %collective-permute-start.41 = (f32[8,128]{1,0:T(8,128)S(1)}, f32[8,128]{1,0:T(8,128)S(1)}, u32[]{:S(2)}, u32[]{:S(2)}) collective-permute-start(f32[8,128]{1,0:T(8,128)S(1)} %norm_sums.1), channel_id=1, source_target_pairs={{0,16},{1,17},{2,18},{3,19},{4,20},{5,21},{6,22},{7,23},{8,24},{9,... | collective-permute-start | bytes 12296 | tf_op jit(solution)/shard_map/ppermute | solution.py:44
  (24 other events, 151.0 us)

commit v2 on v1

--- a/solution.py
+++ b/solution.py
@@ -764,9 +764,9 @@
     small = [spread(jnp.stack([gain, shift, b_out, b_down]), 16), spread(b_qkv, 16), spread(b_up, 64)]
     small = jnp.concatenate(small + [jnp.zeros((PAD - 11, 128), BF16)])
     small = small + exchange(small, "c")
-    weights = pack_call(w_qkv.transpose(1, 0, 2), w_up, w_out, w_down, after=(small,))
+    weights = pack_call(w_qkv.transpose(1, 0, 2), w_up, w_out, w_down, after=())
     weights_got = exchange(weights, "z", 0)
-    a, b = begin_call(x, g, after=(small,))
+    a, b = begin_call(x, g, after=(weights,))
     a_got, b_got = exchange(a, "x", 0), exchange(b, "y", 0)
     small = small + exchange(small, "z", 1)
     small, a, b = join([small], both(a, a_got), both(b, b_got), after=(weights_got,))
@@ -812,11 +812,12 @@
     a_got, b_got = exchange(a[2], "y", 1), exchange(b[2], "x", 1)
     keep, *sends = fold_core_call(keep, *got)
     first, last = [exchange(send, "z", 0) for send in sends]
-    a, b, _ = fold_call(4, (a[0], a[1], a_got), (b[0], b[1], b_got))
+    send = fold_row_call(keep, first, ())
+    got = exchange(send, "z", 1)
+    a, b, _ = fold_call(4, (a[0], a[1], a_got), (b[0], b[1], b_got), after=(send,))
     a_got, b_got = exchange(a[2], "x", 0), exchange(b[2], "y", 0)
     a, b, _ = fold_call(2, (a[0], a[1], a_got), (b[0], b[1], b_got))
     a_got, b_got = exchange(a[2], "x", 1), exchange(b[2], "y", 1)
-    got = exchange(fold_row_call(keep, first, (a[0],)), "z", 1)
     sums = norm_sums_call(a[1], a_got, b[1], b_got, centered, after=(last,))
     sums = sums + exchange(sums, "c")
     block_out, input_grad = finish_call(a[0], a[1], a_got, b[0], b[1], b_got, x, g, centered, inv, small)

time: 171 us -> 166 us (0.971)
  starting transfers between devices: 71.4 us -> 61.7 us
  waiting for transfers between devices: 39 us -> 45.5 us
    ppermute x45, starting transfers between devices: 71.4 us -> 61.7 us  [exchange(): return lax.ppermute(value, ('row', 'col'), pairs)]
    ppermute x45, waiting for transfers between devices: 39 us -> 45.5 us  [exchange(): return lax.ppermute(value, ('row', 'col'), pairs)]
  transfers between devices with their start and end apart: 45 -> 45, of which waited for: 18 -> 18; matrix products, arithmetic and copies ran while one was open for 2% -> 2% of each run, Pallas kernels for 30% -> 31%
where the time goes in v2:
time: 166 us
  starting transfers between devices  61.7 us (37%)
  Pallas kernels  52.9 us (32%)
  waiting for transfers between devices  45.5 us (27%)
  between operations  2.4 us (1%)
  other arithmetic  2.16 us (1%)
    ppermute x45, starting transfers between devices, exchange(): return lax.ppermute(value, ('row', 'col'), pairs)  61.7 us
    pallas_call x24, Pallas kernels, call(): pl.pallas_call(kernel, in_specs=specs, out_specs=[vmem()] * len(outs), ou...  52.9 us
    ppermute x45, waiting for transfers between devices, exchange(): return lax.ppermute(value, ('row', 'col'), pairs)  45.5 us
  transfers between devices with their start and end apart: 45, of which 18 were waited for; matrix products, arithmetic and copies ran while one was open for 2% of the time, Pallas kernels for 31%

profile of v2, /device:TPU:1, one launch (start us, length us, event | category | flops | bytes accessed | tf_op | source)
XLA Modules:
  0.0 165.8 jit_solution(18029936146614636854)
XLA Ops:
  2.1 4.7 %collective-permute-start.4 = (bf16[1,256,1536]{2,1,0:T(8,128)(2,1)S(1)}, bf16[1,256,1536]{2,1,0:T(8,128)(2,1)S(1)}, u32[]{:S(2)}, u32[]{:S(2)}) collective-permute-start(bf16[1,256,1536]{2,1,0:T(8,128)(2,1)S(1)} %pack.1.refs_2_.mine), channel_id=1, source_target_pairs={{0,32},{1,33},{2,34},{3,35},{4,36},{5,37},{6,38},{7,39},{8,40},{9,... | collective-permute-start | bytes 2359304 | tf_op jit(solution)/shard_map/ppermute | solution.py:44
  7.9 2.6 %collective-permute-start.2 = (bf16[2,512,128]{2,1,0:T(8,128)(2,1)S(1)}, bf16[2,512,128]{2,1,0:T(8,128)(2,1)S(1)}, u32[]{:S(2)}, u32[]{:S(2)}) collective-permute-start(bf16[2,512,128]{2,1,0:T(8,128)(2,1)S(1)} %get-tuple-element.91.refs_1_.refs_3_), channel_id=1, source_target_pairs={{0,1},{1,0},{2,3},{3,2},{4,5},{5,4},{6,7},{7,6},{8,9},{9,8},{10,11... | collective-permute-start | bytes 786440 | tf_op jit(solution)/shard_map/ppermute | solution.py:44
  10.5 2.7 %collective-permute-start.3 = (bf16[2,512,128]{2,1,0:T(8,128)(2,1)S(1)}, bf16[2,512,128]{2,1,0:T(8,128)(2,1)S(1)}, u32[]{:S(2)}, u32[]{:S(2)}) collective-permute-start(bf16[2,512,128]{2,1,0:T(8,128)(2,1)S(1)} %get-tuple-element.92.refs_5_.refs_7_), channel_id=1, source_target_pairs={{0,4},{1,5},{2,6},{3,7},{4,0},{5,1},{6,2},{7,3},{8,12},{9,13},{10,... | collective-permute-start | bytes 786440 | tf_op jit(solution)/shard_map/ppermute | solution.py:44
  15.1 2.4 %collective-permute-done.1 = bf16[16,128]{1,0:T(8,128)(2,1)S(1)} collective-permute-done((bf16[16,128]{1,0:T(8,128)(2,1)S(1)}, bf16[16,128]{1,0:T(8,128)(2,1)S(1)}, u32[]{:S(2)}, u32[]{:S(2)}) %collective-permute-start.1) | collective-permute-done | bytes 4128 | tf_op jit(solution)/shard_map/ppermute | solution.py:44
  19.0 2.8 %collective-permute-start.5 = (bf16[16,128]{1,0:T(8,128)(2,1)S(1)}, bf16[16,128]{1,0:T(8,128)(2,1)S(1)}, u32[]{:S(2)}, u32[]{:S(2)}) collective-permute-start(bf16[16,128]{1,0:T(8,128)(2,1)S(1)} %get-tuple-element.93), channel_id=1, source_target_pairs={{0,32},{1,33},{2,34},{3,35},{4,36},{5,37},{6,38},{7,39},{8,40},{9,... | collective-permute-start | bytes 12296 | tf_op jit(solution)/shard_map/ppermute | solution.py:44
  22.8 3.3 %collective-permute-done.6.refs_3_.refs_5_ = bf16[4,512,128]{2,1,0:T(8,128)(2,1)S(1)} collective-permute-done((bf16[4,512,128]{2,1,0:T(8,128)(2,1)S(1)}, bf16[4,512,128]{2,1,0:T(8,128)(2,1)S(1)}, u32[]{:S(2)}, u32[]{:S(2)}) %collective-permute-start.6) | collective-permute-done | bytes 524320 | tf_op jit(solution)/shard_map/ppermute | solution.py:44
  26.4 2.5 %collective-permute-start.11 = (bf16[8,512,128]{2,1,0:T(8,128)(2,1)S(1)}, bf16[8,512,128]{2,1,0:T(8,128)(2,1)S(1)}, u32[]{:S(2)}, u32[]{:S(2)}) collective-permute-start(bf16[8,512,128]{2,1,0:T(8,128)(2,1)S(1)} %get-tuple-element.99.refs_2_.refs_6_), channel_id=1, source_target_pairs={{0,4},{1,5},{2,6},{3,7},{4,0},{5,1},{6,2},{7,3},{8,12},{9,13},{10,... | collective-permute-start | bytes 3145736 | tf_op jit(solution)/shard_map/ppermute | solution.py:44
  35.5 5.4 %collective-permute-start.18 = (bf16[2,256,896]{2,1,0:T(8,128)(2,1)S(1)}, bf16[2,256,896]{2,1,0:T(8,128)(2,1)S(1)}, u32[]{:S(2)}, u32[]{:S(2)}) collective-permute-start(bf16[2,256,896]{2,1,0:T(8,128)(2,1)S(1)} %get-tuple-element.98.refs_6_.refs_0_), channel_id=1, source_target_pairs={{0,16},{1,17},{2,18},{3,19},{4,20},{5,21},{6,22},{7,23},{8,24},{9,... | collective-permute-start | bytes 2752520 | tf_op jit(solution)/shard_map/ppermute | solution.py:44
  45.6 3.4 %collective-permute-start.19 = (bf16[2,256,896]{2,1,0:T(8,128)(2,1)S(1)}, bf16[2,256,896]{2,1,0:T(8,128)(2,1)S(1)}, u32[]{:S(2)}, u32[]{:S(2)}) collective-permute-start(bf16[2,256,896]{2,1,0:T(8,128)(2,1)S(1)} %collective-permute-done.9.refs_2_.refs_7_.refs_1_), channel_id=1, source_target_pairs={{0,16},{1,17},{2,18},{3,19},{4,20},{5,21},{6,22},{7,23},{8,24},{9,... | collective-permute-start | bytes 2752520 | tf_op jit(solution)/shard_map/ppermute | solution.py:44
  55.3 2.7 %collective-permute-done.17.refs_5_ = bf16[8,16,128]{2,1,0:T(8,128)(2,1)S(1)} collective-permute-done((bf16[8,16,128]{2,1,0:T(8,128)(2,1)S(1)}, bf16[8,16,128]{2,1,0:T(8,128)(2,1)S(1)}, u32[]{:S(2)}, u32[]{:S(2)}) %collective-permute-start.17) | collective-permute-done | bytes 32800 | tf_op jit(solution)/shard_map/ppermute | solution.py:44
  60.5 2.9 %collective-permute-start.21 = (bf16[2,256,640]{2,1,0:T(8,128)(2,1)S(1)}, bf16[2,256,640]{2,1,0:T(8,128)(2,1)S(1)}, u32[]{:S(2)}, u32[]{:S(2)}) collective-permute-start(bf16[2,256,640]{2,1,0:T(8,128)(2,1)S(1)} %collective-permute-done.13.refs_10_.refs_1_.refs_5_), channel_id=1, source_target_pairs={{0,16},{1,17},{2,18},{3,19},{4,20},{5,21},{6,22},{7,23},{8,24},{9,... | collective-permute-start | bytes 1966088 | tf_op jit(solution)/shard_map/ppermute | solution.py:44
  63.4 9.4 %norm_proj.1 = (bf16[1024,2048]{1,0:T(8,128)(2,1)S(1)}, bf16[1024,384]{1,0:T(8,128)(2,1)S(1)}, f32[1024,512]{1,0:T(8,128)S(1)}, bf16[1024,512]{1,0:T(8,128)(2,1)...) custom-call(bf16[8,512,128]{2,1,0:T(8,128)(2,1)S(1)} %get-tuple-element.102.refs_0_, ...), custom_call_target="tpu_custom_call" | custom-call | flops 2249999872 | tf_op jit(solution)/shard_map/norm_proj/pallas_call | solution.py:131
  72.8 3.3 %attend.1 = (bf16[1024,128]{1,0:T(8,128)(2,1)S(1)}, f32[1024,128]{1,0:T(8,128)S(1)}, f32[1024,128]{1,0:T(8,128)S(1)}) custom-call(s32[1,2]{1,0:T(1,128)S(1)} %copy-done.2, bf16[1024,384]{1,0:T(8,128)(2,1)S(1)} %get-tuple-element.105.qkv_ref), custom_call_target="tpu_custom_call" | custom-call | flops 750000000 | tf_op jit(solution)/shard_map/attend/pallas_call | solution.py:131
  76.1 4.6 %project.1 = (bf16[8,512,128]{2,1,0:T(8,128)(2,1)S(1)}, bf16[8,512,128]{2,1,0:T(8,128)(2,1)S(1)}, bf16[8,512,128]{2,1,0:T(8,128)(2,1)S(1)}, bf16[8,512,128]{2,1,0:T(8,128)(2,1)S(1)}) custom-call(bf16[1024,128]{1,0:T(8,128)(2,1)S(1)} %get-tuple-element.106.att_ref.refs_5_, bf16[1024,512]{1,0:T(8,128)(2,1)S(1)} %get-tuple-element.107.act_ref.refs_6_, ...), custom_call_target="tpu_custom_call" | custom-call | flops 1250000000 | tf_op jit(solution)/shard_map/project/pallas_call | solution.py:131
  82.4 2.8 %collective-permute-start.26 = (bf16[8,512,128]{2,1,0:T(8,128)(2,1)S(1)}, bf16[8,512,128]{2,1,0:T(8,128)(2,1)S(1)}, u32[]{:S(2)}, u32[]{:S(2)}) collective-permute-start(bf16[8,512,128]{2,1,0:T(8,128)(2,1)S(1)} %get-tuple-element.124), channel_id=1, source_target_pairs={{0,1},{1,0},{2,3},{3,2},{4,5},{5,4},{6,7},{7,6},{8,9},{9,8},{10,11... | collective-permute-start | bytes 3145736 | tf_op jit(solution)/shard_map/ppermute | solution.py:44
  85.3 6.1 %upstream.1 = (bf16[1024,2048]{1,0:T(8,128)(2,1)S(1)}, bf16[1024,512]{1,0:T(8,128)(2,1)S(1)}, bf16[1024,128]{1,0:T(8,128)(2,1)S(1)}, f32[8,512]{1,0:T(8,128)S(1)}, f32[8,128]{1,0:T(8,128)S(1)}) custom-call(bf16[8,512,128]{2,1,0:T(8,128)(2,1)S(1)} %get-tuple-element.109.refs_0_, bf16[8,512,128]{2,1,0:T(8,128)(2,1)S(1)} %collective-permute-done.22.refs_1_, ...), custom_call_target="tpu_custom_call" | custom-call | flops 1500000000 | tf_op jit(solution)/shard_map/upstream/pallas_call | solution.py:131
  91.4 5.1 %attend_back.1 = (bf16[1024,384]{1,0:T(8,128)(2,1)S(1)}, f32[8,384]{1,0:T(8,128)S(1)}) custom-call(s32[1,2]{1,0:T(1,128)S(1)} %copy-done.2, bf16[1024,384]{1,0:T(8,128)(2,1)S(1)} %get-tuple-element.105.qkv_ref, bf16[1024,128]{1,0:T(8,128)(2,1)S(1)} %get-tuple-element.112.do_ref, f32[1024,128]{1,0:T(8,128)S(1)} %get-tuple-element.113.exact_ref, ...), custom_call_target="tpu_custom_call" | custom-call | flops 1750000000 | tf_op jit(solution)/shard_map/attend_back/pallas_call | solution.py:131
  96.4 6.5 %downstream.1 = (bf16[8,528,128]{2,1,0:T(8,128)(2,1)S(1)}, bf16[8,528,128]{2,1,0:T(8,128)(2,1)S(1)}, bf16[8,528,128]{2,1,0:T(8,128)(2,1)S(1)}, bf16[8,528,128]{2,1,0:T(8,128)(2,1)S(1)}) custom-call(bf16[1024,384]{1,0:T(8,128)(2,1)S(1)} %get-tuple-element.115.dm_ref.refs_1_, bf16[1024,512]{1,0:T(8,128)(2,1)S(1)} %get-tuple-element.116.dh_ref.refs_2_, ...), custom_call_target="tpu_custom_call" | custom-call | flops 1500000000 | tf_op jit(solution)/shard_map/downstream/pallas_call | solution.py:131
  105.1 9.2 %grads.1 = (bf16[4,3264,128]{2,1,0:T(8,128)(2,1)S(1)}, bf16[4,816,128]{2,1,0:T(8,128)(2,1)S(1)}, bf16[4,816,128]{2,1,0:T(8,128)(2,1)S(1)}, bf16[4,816,128]{2,1,0:T(8,128)(2,1)S(1)}, bf16[4,816,128]{2,1,0:T(8,128)(2,1)S(1)}) custom-call(bf16[1024,2048]{1,0:T(8,128)(2,1)S(1)} %get-tuple-element.117.normed_ref.refs_0_, ...), custom_call_target="tpu_custom_call" | custom-call | flops 2750000128 | tf_op jit(solution)/shard_map/grads/pallas_call | solution.py:131
  115.0 3.2 %collective-permute-done.25.refs_3_ = bf16[8,528,128]{2,1,0:T(8,128)(2,1)S(1)} collective-permute-done((bf16[8,528,128]{2,1,0:T(8,128)(2,1)S(1)}, bf16[8,528,128]{2,1,0:T(8,128)(2,1)S(1)}, u32[]{:S(2)}, u32[]{:S(2)}) %collective-permute-start.25) | collective-permute-done | bytes 1081376 | tf_op jit(solution)/shard_map/ppermute | solution.py:44
  124.8 10.2 %collective-permute-done.34.got_ref = bf16[1,3264,128]{2,1,0:T(8,128)(2,1)S(1)} collective-permute-done((bf16[1,3264,128]{2,1,0:T(8,128)(2,1)S(1)}, bf16[1,3264,128]{2,1,0:T(8,128)(2,1)S(1)}, u32[]{:S(2)}, u32[]{:S(2)}) %collective-permute-start.34) | collective-permute-done | bytes 835616 | tf_op jit(solution)/shard_map/ppermute | solution.py:44
  138.9 6.6 %collective-permute-done.35.refs_2_ = bf16[2080,128]{1,0:T(8,128)(2,1)S(1)} collective-permute-done((bf16[2080,128]{1,0:T(8,128)(2,1)S(1)}, bf16[2080,128]{1,0:T(8,128)(2,1)S(1)}, u32[]{:S(2)}, u32[]{:S(2)}) %collective-permute-start.35) | collective-permute-done | bytes 532512 | tf_op jit(solution)/shard_map/ppermute | solution.py:44
  147.4 5.4 %collective-permute-done.37.ga.refs_1_ = bf16[1040,128]{1,0:T(8,128)(2,1)S(1)} collective-permute-done((bf16[1040,128]{1,0:T(8,128)(2,1)S(1)}, bf16[1040,128]{1,0:T(8,128)(2,1)S(1)}, u32[]{:S(2)}, u32[]{:S(2)}) %collective-permute-start.37) | collective-permute-done | bytes 266272 | tf_op jit(solution)/shard_map/ppermute | solution.py:44
  153.1 5.4 %collective-permute-start.41 = (f32[8,128]{1,0:T(8,128)S(1)}, f32[8,128]{1,0:T(8,128)S(1)}, u32[]{:S(2)}, u32[]{:S(2)}) collective-permute-start(f32[8,128]{1,0:T(8,128)S(1)} %norm_sums.1), channel_id=1, source_target_pairs={{0,16},{1,17},{2,18},{3,19},{4,20},{5,21},{6,22},{7,23},{8,24},{9,... | collective-permute-start | bytes 12296 | tf_op jit(solution)/shard_map/ppermute | solution.py:44
  (133 shorter events, 50.2 us)
Async XLA Ops:
  2.1 15.5 %collective-permute-start.4 = (bf16[1,256,1536]{2,1,0:T(8,128)(2,1)S(1)}, bf16[1,256,1536]{2,1,0:T(8,128)(2,1)S(1)}, u32[]{:S(2)}, u32[]{:S(2)}) collective-permute-start(bf16[1,256,1536]{2,1,0:T(8,128)(2,1)S(1)} %pack.1.refs_2_.mine), channel_id=1, source_target_pairs={{0,32},{1,33},{2,34},{3,35},{4,36},{5,37},{6,38},{7,39},{8,40},{9,... | collective-permute-start | bytes 2359304 | tf_op jit(solution)/shard_map/ppermute | solution.py:44
  7.9 9.7 %collective-permute-start.2 = (bf16[2,512,128]{2,1,0:T(8,128)(2,1)S(1)}, bf16[2,512,128]{2,1,0:T(8,128)(2,1)S(1)}, u32[]{:S(2)}, u32[]{:S(2)}) collective-permute-start(bf16[2,512,128]{2,1,0:T(8,128)(2,1)S(1)} %get-tuple-element.91.refs_1_.refs_3_), channel_id=1, source_target_pairs={{0,1},{1,0},{2,3},{3,2},{4,5},{5,4},{6,7},{7,6},{8,9},{9,8},{10,11... | collective-permute-start | bytes 786440 | tf_op jit(solution)/shard_map/ppermute | solution.py:44
  18.9 21.9 %collective-permute-start.9 = (bf16[2,256,896]{2,1,0:T(8,128)(2,1)S(1)}, bf16[2,256,896]{2,1,0:T(8,128)(2,1)S(1)}, u32[]{:S(2)}, u32[]{:S(2)}) collective-permute-start(bf16[2,256,896]{2,1,0:T(8,128)(2,1)S(1)} %get-tuple-element.98.refs_6_.refs_0_), channel_id=1, source_target_pairs={{0,96},{1,97},{2,98},{3,99},{4,100},{5,101},{6,102},{7,103},{8,104... | collective-permute-start | bytes 2752520 | tf_op jit(solution)/shard_map/ppermute | solution.py:44
  26.4 17.9 %collective-permute-start.11 = (bf16[8,512,128]{2,1,0:T(8,128)(2,1)S(1)}, bf16[8,512,128]{2,1,0:T(8,128)(2,1)S(1)}, u32[]{:S(2)}, u32[]{:S(2)}) collective-permute-start(bf16[8,512,128]{2,1,0:T(8,128)(2,1)S(1)} %get-tuple-element.99.refs_2_.refs_6_), channel_id=1, source_target_pairs={{0,4},{1,5},{2,6},{3,7},{4,0},{5,1},{6,2},{7,3},{8,12},{9,13},{10,... | collective-permute-start | bytes 3145736 | tf_op jit(solution)/shard_map/ppermute | solution.py:44
  28.9 15.3 %collective-permute-start.12 = (bf16[8,512,128]{2,1,0:T(8,128)(2,1)S(1)}, bf16[8,512,128]{2,1,0:T(8,128)(2,1)S(1)}, u32[]{:S(2)}, u32[]{:S(2)}) collective-permute-start(bf16[8,512,128]{2,1,0:T(8,128)(2,1)S(1)} %get-tuple-element.100.refs_4_.refs_8_), channel_id=1, source_target_pairs={{0,1},{1,0},{2,3},{3,2},{4,5},{5,4},{6,7},{7,6},{8,9},{9,8},{10,11... | collective-permute-start | bytes 3145736 | tf_op jit(solution)/shard_map/ppermute | solution.py:44
  31.3 12.9 %collective-permute-start.13 = (bf16[2,256,640]{2,1,0:T(8,128)(2,1)S(1)}, bf16[2,256,640]{2,1,0:T(8,128)(2,1)S(1)}, u32[]{:S(2)}, u32[]{:S(2)}) collective-permute-start(bf16[2,256,640]{2,1,0:T(8,128)(2,1)S(1)} %get-tuple-element.101.refs_0_.refs_4_), channel_id=1, source_target_pairs={{0,96},{1,97},{2,98},{3,99},{4,100},{5,101},{6,102},{7,103},{8,104... | collective-permute-start | bytes 1966088 | tf_op jit(solution)/shard_map/ppermute | solution.py:44
  35.5 19.8 %collective-permute-start.18 = (bf16[2,256,896]{2,1,0:T(8,128)(2,1)S(1)}, bf16[2,256,896]{2,1,0:T(8,128)(2,1)S(1)}, u32[]{:S(2)}, u32[]{:S(2)}) collective-permute-start(bf16[2,256,896]{2,1,0:T(8,128)(2,1)S(1)} %get-tuple-element.98.refs_6_.refs_0_), channel_id=1, source_target_pairs={{0,16},{1,17},{2,18},{3,19},{4,20},{5,21},{6,22},{7,23},{8,24},{9,... | collective-permute-start | bytes 2752520 | tf_op jit(solution)/shard_map/ppermute | solution.py:44
  44.5 16.0 %collective-permute-start.14 = (bf16[8,512,128]{2,1,0:T(8,128)(2,1)S(1)}, bf16[8,512,128]{2,1,0:T(8,128)(2,1)S(1)}, u32[]{:S(2)}, u32[]{:S(2)}) collective-permute-start(bf16[8,512,128]{2,1,0:T(8,128)(2,1)S(1)} %get-tuple-element.102.refs_0_), channel_id=1, source_target_pairs={{0,12},{1,13},{2,14},{3,15},{4,8},{5,9},{6,10},{7,11},{8,4},{9,5},... | collective-permute-start | bytes 3145736 | tf_op jit(solution)/shard_map/ppermute | solution.py:44
  45.6 12.8 %collective-permute-start.19 = (bf16[2,256,896]{2,1,0:T(8,128)(2,1)S(1)}, bf16[2,256,896]{2,1,0:T(8,128)(2,1)S(1)}, u32[]{:S(2)}, u32[]{:S(2)}) collective-permute-start(bf16[2,256,896]{2,1,0:T(8,128)(2,1)S(1)} %collective-permute-done.9.refs_2_.refs_7_.refs_1_), channel_id=1, source_target_pairs={{0,16},{1,17},{2,18},{3,19},{4,20},{5,21},{6,22},{7,23},{8,24},{9,... | collective-permute-start | bytes 2752520 | tf_op jit(solution)/shard_map/ppermute | solution.py:44
  49.0 14.4 %collective-permute-start.15 = (bf16[8,512,128]{2,1,0:T(8,128)(2,1)S(1)}, bf16[8,512,128]{2,1,0:T(8,128)(2,1)S(1)}, u32[]{:S(2)}, u32[]{:S(2)}) collective-permute-start(bf16[8,512,128]{2,1,0:T(8,128)(2,1)S(1)} %get-tuple-element.103.refs_2_), channel_id=1, source_target_pairs={{0,3},{1,2},{2,1},{3,0},{4,7},{5,6},{6,5},{7,4},{8,11},{9,10},{10,... | collective-permute-start | bytes 3145736 | tf_op jit(solution)/shard_map/ppermute | solution.py:44
  55.3 30.0 %collective-permute-start.22 = (bf16[8,512,128]{2,1,0:T(8,128)(2,1)S(1)}, bf16[8,512,128]{2,1,0:T(8,128)(2,1)S(1)}, u32[]{:S(2)}, u32[]{:S(2)}) collective-permute-start(bf16[8,512,128]{2,1,0:T(8,128)(2,1)S(1)} %get-tuple-element.109.refs_0_), channel_id=1, source_target_pairs={{0,12},{1,13},{2,14},{3,15},{4,8},{5,9},{6,10},{7,11},{8,4},{9,5},... | collective-permute-start | bytes 3145736 | tf_op jit(solution)/shard_map/ppermute | solution.py:44
  58.0 27.3 %collective-permute-start.23 = (bf16[8,512,128]{2,1,0:T(8,128)(2,1)S(1)}, bf16[8,512,128]{2,1,0:T(8,128)(2,1)S(1)}, u32[]{:S(2)}, u32[]{:S(2)}) collective-permute-start(bf16[8,512,128]{2,1,0:T(8,128)(2,1)S(1)} %get-tuple-element.110.refs_2_), channel_id=1, source_target_pairs={{0,3},{1,2},{2,1},{3,0},{4,7},{5,6},{6,5},{7,4},{8,11},{9,10},{10,... | collective-permute-start | bytes 3145736 | tf_op jit(solution)/shard_map/ppermute | solution.py:44
  58.4 17.6 %collective-permute-start.20 = (bf16[2,256,640]{2,1,0:T(8,128)(2,1)S(1)}, bf16[2,256,640]{2,1,0:T(8,128)(2,1)S(1)}, u32[]{:S(2)}, u32[]{:S(2)}) collective-permute-start(bf16[2,256,640]{2,1,0:T(8,128)(2,1)S(1)} %get-tuple-element.101.refs_0_.refs_4_), channel_id=1, source_target_pairs={{0,16},{1,17},{2,18},{3,19},{4,20},{5,21},{6,22},{7,23},{8,24},{9,... | collective-permute-start | bytes 1966088 | tf_op jit(solution)/shard_map/ppermute | solution.py:44
  60.5 15.5 %collective-permute-start.21 = (bf16[2,256,640]{2,1,0:T(8,128)(2,1)S(1)}, bf16[2,256,640]{2,1,0:T(8,128)(2,1)S(1)}, u32[]{:S(2)}, u32[]{:S(2)}) collective-permute-start(bf16[2,256,640]{2,1,0:T(8,128)(2,1)S(1)} %collective-permute-done.13.refs_10_.refs_1_.refs_5_), channel_id=1, source_target_pairs={{0,16},{1,17},{2,18},{3,19},{4,20},{5,21},{6,22},{7,23},{8,24},{9,... | collective-permute-start | bytes 1966088 | tf_op jit(solution)/shard_map/ppermute | solution.py:44
  80.7 24.4 %collective-permute-start.24 = (bf16[8,512,128]{2,1,0:T(8,128)(2,1)S(1)}, bf16[8,512,128]{2,1,0:T(8,128)(2,1)S(1)}, u32[]{:S(2)}, u32[]{:S(2)}) collective-permute-start(bf16[8,512,128]{2,1,0:T(8,128)(2,1)S(1)} %get-tuple-element.120), channel_id=1, source_target_pairs={{0,4},{1,5},{2,6},{3,7},{4,0},{5,1},{6,2},{7,3},{8,12},{9,13},{10,... | collective-permute-start | bytes 3145736 | tf_op jit(solution)/shard_map/ppermute | solution.py:44
  82.4 22.6 %collective-permute-start.26 = (bf16[8,512,128]{2,1,0:T(8,128)(2,1)S(1)}, bf16[8,512,128]{2,1,0:T(8,128)(2,1)S(1)}, u32[]{:S(2)}, u32[]{:S(2)}) collective-permute-start(bf16[8,512,128]{2,1,0:T(8,128)(2,1)S(1)} %get-tuple-element.124), channel_id=1, source_target_pairs={{0,1},{1,0},{2,3},{3,2},{4,5},{5,4},{6,7},{7,6},{8,9},{9,8},{10,11... | collective-permute-start | bytes 3145736 | tf_op jit(solution)/shard_map/ppermute | solution.py:44
  102.9 15.3 %collective-permute-start.25 = (bf16[8,528,128]{2,1,0:T(8,128)(2,1)S(1)}, bf16[8,528,128]{2,1,0:T(8,128)(2,1)S(1)}, u32[]{:S(2)}, u32[]{:S(2)}) collective-permute-start(bf16[8,528,128]{2,1,0:T(8,128)(2,1)S(1)} %get-tuple-element.121), channel_id=1, source_target_pairs={{0,4},{1,5},{2,6},{3,7},{4,0},{5,1},{6,2},{7,3},{8,12},{9,13},{10,... | collective-permute-start | bytes 3244040 | tf_op jit(solution)/shard_map/ppermute | solution.py:44
  105.0 15.2 %collective-permute-start.27 = (bf16[8,528,128]{2,1,0:T(8,128)(2,1)S(1)}, bf16[8,528,128]{2,1,0:T(8,128)(2,1)S(1)}, u32[]{:S(2)}, u32[]{:S(2)}) collective-permute-start(bf16[8,528,128]{2,1,0:T(8,128)(2,1)S(1)} %get-tuple-element.125), channel_id=1, source_target_pairs={{0,1},{1,0},{2,3},{3,2},{4,5},{5,4},{6,7},{7,6},{8,9},{9,8},{10,11... | collective-permute-start | bytes 3244040 | tf_op jit(solution)/shard_map/ppermute | solution.py:44
  121.1 14.2 %collective-permute-start.28 = (bf16[4160,128]{1,0:T(8,128)(2,1)S(1)}, bf16[4160,128]{1,0:T(8,128)(2,1)S(1)}, u32[]{:S(2)}, u32[]{:S(2)}) collective-permute-start(bf16[4160,128]{1,0:T(8,128)(2,1)S(1)} %get-tuple-element.128), channel_id=1, source_target_pairs={{0,12},{1,13},{2,14},{3,15},{4,8},{5,9},{6,10},{7,11},{8,4},{9,5},... | collective-permute-start | bytes 3194888 | tf_op jit(solution)/shard_map/ppermute | solution.py:44
  121.3 14.2 %collective-permute-start.29 = (bf16[4160,128]{1,0:T(8,128)(2,1)S(1)}, bf16[4160,128]{1,0:T(8,128)(2,1)S(1)}, u32[]{:S(2)}, u32[]{:S(2)}) collective-permute-start(bf16[4160,128]{1,0:T(8,128)(2,1)S(1)} %get-tuple-element.131), channel_id=1, source_target_pairs={{0,3},{1,2},{2,1},{3,0},{4,7},{5,6},{6,5},{7,4},{8,11},{9,10},{10,... | collective-permute-start | bytes 3194888 | tf_op jit(solution)/shard_map/ppermute | solution.py:44
  122.1 13.0 %collective-permute-start.34 = (bf16[1,3264,128]{2,1,0:T(8,128)(2,1)S(1)}, bf16[1,3264,128]{2,1,0:T(8,128)(2,1)S(1)}, u32[]{:S(2)}, u32[]{:S(2)}) collective-permute-start(bf16[1,3264,128]{2,1,0:T(8,128)(2,1)S(1)} %get-tuple-element.142), channel_id=1, source_target_pairs={{0,32},{1,33},{2,34},{3,35},{4,36},{5,37},{6,38},{7,39},{8,40},{9,... | collective-permute-start | bytes 2506760 | tf_op jit(solution)/shard_map/ppermute | solution.py:44
  123.1 24.3 %collective-permute-start.39 = (bf16[1,3264,128]{2,1,0:T(8,128)(2,1)S(1)}, bf16[1,3264,128]{2,1,0:T(8,128)(2,1)S(1)}, u32[]{:S(2)}, u32[]{:S(2)}) collective-permute-start(bf16[1,3264,128]{2,1,0:T(8,128)(2,1)S(1)} %get-tuple-element.159), channel_id=1, source_target_pairs={{0,32},{1,33},{2,34},{3,35},{4,36},{5,37},{6,38},{7,39},{8,40},{9,... | collective-permute-start | bytes 2506760 | tf_op jit(solution)/shard_map/ppermute | solution.py:44
  135.2 28.7 %collective-permute-start.40 = (bf16[1,3264,128]{2,1,0:T(8,128)(2,1)S(1)}, bf16[1,3264,128]{2,1,0:T(8,128)(2,1)S(1)}, u32[]{:S(2)}, u32[]{:S(2)}) collective-permute-start(bf16[1,3264,128]{2,1,0:T(8,128)(2,1)S(1)} %fold_row.1.refs_6_), channel_id=1, source_target_pairs={{0,96},{1,97},{2,98},{3,99},{4,100},{5,101},{6,102},{7,103},{8,104... | collective-permute-start | bytes 2506760 | tf_op jit(solution)/shard_map/ppermute | solution.py:44
  135.8 9.7 %collective-permute-start.35 = (bf16[2080,128]{1,0:T(8,128)(2,1)S(1)}, bf16[2080,128]{1,0:T(8,128)(2,1)S(1)}, u32[]{:S(2)}, u32[]{:S(2)}) collective-permute-start(bf16[2080,128]{1,0:T(8,128)(2,1)S(1)} %get-tuple-element.145), channel_id=1, source_target_pairs={{0,1},{1,0},{2,3},{3,2},{4,5},{5,4},{6,7},{7,6},{8,9},{9,8},{10,11... | collective-permute-start | bytes 1597448 | tf_op jit(solution)/shard_map/ppermute | solution.py:44
  (30 other events, 211.2 us)
